TPU v7x, 32 devices: a whole 2x2x4 slice. The times are simulated.
32 devices in a mesh: dp: 2 (over x), segment: 16 (over z, y, core).
Axes of the slice: x: 2, y: 2, z: 4, core: 2. Of those that a mesh axis runs over, the one named last changes fastest.
Arguments:
- feed_rising: bfloat16 [4, 128, 512], P(None, 'dp'), may hold values from -6 to 6
- feed_falling: bfloat16 [4, 128, 512], P(None, 'dp'), may hold values from -6 to 6
- up_weight: bfloat16 [32, 512, 1024], P('segment'), as said below
- down_weight: bfloat16 [32, 1024, 512], P('segment'), as said below
- norm_gain: float32 [32, 512], P('segment'), as said below
Outputs:
- grad_up: float32 [512, 8192], P('dp', 'segment')
- grad_down: float32 [8192, 512], P('segment', 'dp')
- grad_gain: float32 [16, 256], P('segment', 'dp')
Inputs may be any that keep to these rules, and one draw needn't show every extreme that they name: `up_weight`: normal entries of standard deviation 512^-0.5; the rows of one section (2i, 2i + 1 as in the meaning) are equal. `down_weight`: normal entries of standard deviation 1024^-0.5; the rows of one section are equal. `norm_gain`: the rows of one section are equal.
All inputs are finite; a program needn't handle non-finite values.
Results may differ from a plain program's by a relative error of at most 0.011.
Values may be sent and summed in bfloat16 or wider, within the bound.
A program may use at most 64 MiB of HBM per device.

v0:
```python
import math

import jax
import jax.numpy as jnp
from jax import lax
from jax.sharding import PartitionSpec as P

GELU_C = 0.7978845608028654
CUBIC = 0.044715


def for_sending(shard):
    return jax.tree.map(lambda a: a.astype(jnp.bfloat16) if a.dtype == jnp.float32 else a, shard)


def passed_along(block, axis, distance):
    devices = range(lax.axis_size(axis))
    route = [(i - distance, i) for i in devices if i - distance in devices]
    return lax.ppermute(block, axis, route)


def partner(shard, axis, stride):
    return lax.ppermute(shard, axis, [(i, i ^ 1 << stride) for i in range(lax.axis_size(axis))])


def gelu_parts(pre_act):
    inner_arg = GELU_C * (pre_act + CUBIC * pre_act * pre_act * pre_act)
    tangent = jnp.tanh(inner_arg)
    gelu_value = 0.5 * pre_act * (1.0 + tangent)
    gelu_slope = 0.5 * (1.0 + tangent) + 0.5 * pre_act * (1.0 - tangent * tangent) * GELU_C * (
        1.0 + 3.0 * CUBIC * pre_act * pre_act
    )
    return (gelu_value, gelu_slope)


def norm_parts(activations, gain_row):
    values = activations.astype(jnp.float32)
    centre = jnp.mean(values, axis=-1, keepdims=True)
    spread = jnp.mean(jnp.square(values - centre), axis=-1, keepdims=True)
    inverse = lax.rsqrt(spread + 1e-05)
    normed = (values - centre) * inverse
    return (normed, inverse, (normed * gain_row).astype(jnp.bfloat16))


def move_rising(block_rows):
    return jax.tree.map(
        lambda part, own: part.astype(own.dtype),
        passed_along(for_sending(block_rows), "segment", 2),
        block_rows,
    )


def move_falling(block_rows):
    return jax.tree.map(
        lambda part, own: part.astype(own.dtype),
        passed_along(for_sending(block_rows), "segment", -2),
        block_rows,
    )


def put_slot(stack, slot, update, valid):
    previous = lax.dynamic_index_in_dim(stack, slot, 0, keepdims=False)
    chosen = jnp.where(valid, update, previous)
    return lax.dynamic_update_index_in_dim(stack, chosen, slot, 0)


def take_half(grads, which, half_units):
    up_part = lax.dynamic_slice_in_dim(grads[0], which * half_units, half_units, 1)
    down_part = lax.dynamic_slice_in_dim(grads[1], which * half_units, half_units, 0)
    gain_part = lax.dynamic_slice_in_dim(grads[2], which, 1, 0)
    return (up_part, down_part, gain_part)


def add_three(first, second):
    return (first[0] + second[0], first[1] + second[1], first[2] + second[2])


def body(feed_rising, feed_falling, up_weight, down_weight, norm_gain):
    segments = lax.axis_size("segment")
    place = lax.axis_index("segment")
    pair_index = place // 2
    core_bit = place % 2
    sections = segments // 2
    micro = feed_rising.shape[0]
    local_rows = feed_rising.shape[1] // 2
    width = feed_rising.shape[2]
    hidden_units = up_weight.shape[2]
    loss_scale = 1.0 / math.sqrt(2.0 * micro * feed_rising.shape[1] * lax.axis_size("dp"))
    ticks = micro + sections - 1
    own_feeds = (
        lax.dynamic_slice_in_dim(feed_rising, core_bit * local_rows, local_rows, 1),
        lax.dynamic_slice_in_dim(feed_falling, core_bit * local_rows, local_rows, 1),
    )
    entry_pair = (0, sections - 1)
    exit_pair = (sections - 1, 0)
    forward_start = (pair_index, sections - 1 - pair_index)
    backward_start = (sections - 1 - pair_index, pair_index)
    zero_rows = jnp.zeros((local_rows, width), jnp.bfloat16)
    zero_stack = jnp.zeros((micro, local_rows, width), jnp.bfloat16)
    zero_pre = jnp.zeros((micro, local_rows, hidden_units), jnp.float32)
    zero_hidden = jnp.zeros((micro, local_rows, hidden_units), jnp.bfloat16)
    empty_store = (zero_stack, zero_stack, zero_pre, zero_hidden, zero_stack)

    def forward_tick(tick, state):
        carried, stores = state
        emitted_pair = []
        new_stores = []
        for role in (0, 1):
            slot = tick - forward_start[role]
            valid = (slot >= 0) & (slot < micro)
            slot_c = jnp.clip(slot, 0, micro - 1)
            fresh = lax.dynamic_index_in_dim(own_feeds[role], slot_c, 0, keepdims=False)
            rows_in = jnp.where(pair_index == entry_pair[role], fresh, carried[role])
            normed, inverse, normed_b = norm_parts(rows_in, norm_gain[role])
            pre_act = jnp.dot(normed_b, up_weight[role], preferred_element_type=jnp.float32)
            gelu_value, gelu_slope = gelu_parts(pre_act)
            hidden = gelu_value.astype(jnp.bfloat16)
            emitted = (
                rows_in.astype(jnp.float32)
                + jnp.dot(hidden, down_weight[role], preferred_element_type=jnp.float32)
            ).astype(jnp.bfloat16)
            input_store, normed_store, pre_store, hidden_store, final_store = stores[role]
            input_store = put_slot(input_store, slot_c, rows_in, valid)
            normed_store = put_slot(normed_store, slot_c, normed_b, valid)
            pre_store = put_slot(pre_store, slot_c, pre_act, valid)
            hidden_store = put_slot(hidden_store, slot_c, hidden, valid)
            final_store = put_slot(
                final_store, slot_c, emitted, valid & (pair_index == exit_pair[role])
            )
            new_stores.append((input_store, normed_store, pre_store, hidden_store, final_store))
            emitted_pair.append(emitted)
        next_carried = (move_rising(emitted_pair[0]), move_falling(emitted_pair[1]))
        return (next_carried, (new_stores[0], new_stores[1]))

    carried, stores = lax.fori_loop(
        0, ticks, forward_tick, ((zero_rows, zero_rows), (empty_store, empty_store))
    )
    zero_gain = jnp.zeros((width,), jnp.float32)

    def backward_tick(tick, state):
        carried, cot_stores, grad_stores, gain_sums = state
        sent_pair = []
        new_cots = []
        new_grads = []
        new_gains = []
        for role in (0, 1):
            input_store, normed_store, pre_store, hidden_store, final_store = stores[role]
            slot = tick - backward_start[role]
            valid = (slot >= 0) & (slot < micro)
            slot_c = jnp.clip(slot, 0, micro - 1)
            final_rows = lax.dynamic_index_in_dim(final_store, slot_c, 0, keepdims=False)
            fresh = (final_rows.astype(jnp.float32) * loss_scale).astype(jnp.bfloat16)
            incoming = jnp.where(pair_index == exit_pair[role], fresh, carried[role])
            incoming = jnp.where(valid, incoming, jnp.zeros_like(incoming))
            rows_in = lax.dynamic_index_in_dim(input_store, slot_c, 0, keepdims=False)
            normed, inverse, normed_b = norm_parts(rows_in, norm_gain[role])
            pre_act = lax.dynamic_index_in_dim(pre_store, slot_c, 0, keepdims=False)
            gelu_value, gelu_slope = gelu_parts(pre_act)
            back_hidden = lax.dot_general(
                incoming,
                down_weight[role],
                (((1,), (1,)), ((), ())),
                preferred_element_type=jnp.float32,
            )
            pre_grad = (back_hidden * gelu_slope).astype(jnp.bfloat16)
            back_norm = lax.dot_general(
                pre_grad,
                up_weight[role],
                (((1,), (1,)), ((), ())),
                preferred_element_type=jnp.float32,
            )
            new_gains.append(gain_sums[role] + jnp.sum(back_norm * normed, axis=0))
            scaled = back_norm * norm_gain[role]
            first_mean = jnp.mean(scaled, axis=-1, keepdims=True)
            second_mean = jnp.mean(scaled * normed, axis=-1, keepdims=True)
            sent = (
                incoming.astype(jnp.float32)
                + inverse * (scaled - first_mean - normed * second_mean)
            ).astype(jnp.bfloat16)
            new_cots.append(put_slot(cot_stores[role], slot_c, incoming, valid))
            new_grads.append(put_slot(grad_stores[role], slot_c, pre_grad, valid))
            sent_pair.append(sent)
        next_carried = (move_falling(sent_pair[0]), move_rising(sent_pair[1]))
        return (
            next_carried,
            (new_cots[0], new_cots[1]),
            (new_grads[0], new_grads[1]),
            (new_gains[0], new_gains[1]),
        )

    start_state = (
        (zero_rows, zero_rows),
        (zero_stack, zero_stack),
        (zero_hidden, zero_hidden),
        (zero_gain, zero_gain),
    )
    carried, cot_stores, grad_stores, gain_sums = lax.fori_loop(
        0, ticks, backward_tick, start_state
    )
    partials = []
    for role in (0, 1):
        normed_store = stores[role][1]
        hidden_store = stores[role][3]
        part_up = jnp.einsum(
            "mrd,mrh->dh", normed_store, grad_stores[role], preferred_element_type=jnp.float32
        ).astype(jnp.bfloat16)
        part_down = jnp.einsum(
            "mrh,mrd->hd", hidden_store, cot_stores[role], preferred_element_type=jnp.float32
        ).astype(jnp.bfloat16)
        part_gain = gain_sums[role].astype(jnp.bfloat16).reshape(2, width // 2)
        partials.extend([part_up, part_down, part_gain])
    summed = (
        lax.psum_scatter(partials[0], "dp", scatter_dimension=0, tiled=True).astype(jnp.float32),
        lax.psum_scatter(partials[1], "dp", scatter_dimension=1, tiled=True).astype(jnp.float32),
        lax.psum_scatter(partials[2], "dp", scatter_dimension=1, tiled=True).astype(jnp.float32),
        lax.psum_scatter(partials[3], "dp", scatter_dimension=0, tiled=True).astype(jnp.float32),
        lax.psum_scatter(partials[4], "dp", scatter_dimension=1, tiled=True).astype(jnp.float32),
        lax.psum_scatter(partials[5], "dp", scatter_dimension=1, tiled=True).astype(jnp.float32),
    )
    first_held = (summed[0], summed[1], summed[2])
    second_held = (summed[3], summed[4], summed[5])
    half_units = hidden_units // 2
    bit_count = segments.bit_length() - 1
    bit_list = list(range(0, bit_count))
    travelling = second_held
    for bit in bit_list:
        travelling = (
            partner(travelling[0].astype(jnp.bfloat16), "segment", bit).astype(jnp.float32),
            partner(travelling[1].astype(jnp.bfloat16), "segment", bit).astype(jnp.float32),
            partner(travelling[2].astype(jnp.bfloat16), "segment", bit).astype(jnp.float32),
        )
    section_sums = add_three(first_held, travelling)
    keep_part = take_half(section_sums, core_bit, half_units)
    give_part = take_half(section_sums, 1 - core_bit, half_units)
    received = partner(
        (for_sending(give_part[0]), for_sending(give_part[1]), for_sending(give_part[2])),
        "segment",
        0,
    )
    result = add_three(keep_part, received)
    return (result[0], result[1], result[2])


def solution(mesh):
    return jax.shard_map(
        body,
        mesh=mesh,
        in_specs=(
            P(None, "dp", None),
            P(None, "dp", None),
            P("segment", None, None),
            P("segment", None, None),
            P("segment", None),
        ),
        out_specs=(P("dp", "segment"), P("segment", "dp"), P("segment", "dp")),
        check_vma=False,
    )
```

profile of v0, /device:TPU:0, one launch (start us, length us, event | category | flops | bytes accessed | tf_op | source)
XLA Modules:
  0.0 617.4 jit_solution(17564418403891042721)
XLA Ops:
  12.9 198.1 %while.65 = (s32[]{:T(128)}, bf16[32,512]{1,0:T(8,128)(2,1)S(1)}, bf16[32,512]{1,0:T(8,128)(2,1)S(1)}, bf16[4,32,512]{2,1,0:T(8,128)(2,1)S(1)}, bf16[4,32,512]{2...) while((s32[]{:T(128)}, bf16[32,512]{1,0:T(8,128)(2,1)S(1)}, ...), condition=%wide.region_5.6_spmd, body=%wide.region_0.5_spmd.sunk | while | flops 136282176 | bytes 16601893 | solution.py:135
  20.8 5.5 collective-permute-start
  38.8 5.5 collective-permute-start
  56.8 5.4 collective-permute-start
  74.8 5.5 collective-permute-start
  92.9 5.4 collective-permute-start
  110.9 5.4 collective-permute-start
  128.9 5.4 collective-permute-start
  146.9 5.4 collective-permute-start
  164.9 5.4 collective-permute-start
  182.9 5.4 collective-permute-start
  200.9 5.4 collective-permute-start
  214.4 269.8 %while.66 = (s32[]{:T(128)}, bf16[32,512]{1,0:T(8,128)(2,1)S(1)}, bf16[32,512]{1,0:T(8,128)(2,1)}, bf16[4,32,512]{2,1,0:T(8,128)(2,1)}, bf16[4,32,512]{2,1,0:T(8...) while((s32[]{:T(128)}, bf16[32,512]{1,0:T(8,128)(2,1)S(1)}, ...), condition=%wide.region_17.18_spmd.clone, body=%wide.region_6.17_spmd.clone.sunk | while | flops 136578112 | bytes 6734593 | solution.py:197
  217.6 2.3 bitcast_dynamic-update-slice_fusion.37
  222.3 6.2 collective-permute-start.3
  231.6 2.3 bitcast_dynamic-update-slice_fusion.35
  237.1 3.9 collective-permute-done.2
  248.7 3.7 collective-permute-start.3
  255.6 2.3 bitcast_dynamic-update-slice_fusion.35
  261.7 3.2 collective-permute-done.2
  268.1 2.3 bitcast_dynamic-update-slice_fusion.37
  272.8 5.6 collective-permute-start.3
  281.4 2.3 bitcast_dynamic-update-slice_fusion.35
  287.6 3.2 collective-permute-done.2
  298.6 3.7 collective-permute-start.3
  305.4 2.3 bitcast_dynamic-update-slice_fusion.35
  311.6 3.2 collective-permute-done.2
  317.9 2.3 bitcast_dynamic-update-slice_fusion.37
  322.6 5.6 collective-permute-start.3
  331.3 2.3 bitcast_dynamic-update-slice_fusion.35
  337.5 3.2 collective-permute-done.2
  343.8 2.3 bitcast_dynamic-update-slice_fusion.37
  348.5 3.7 collective-permute-start.3
  355.2 2.3 bitcast_dynamic-update-slice_fusion.35
  361.4 3.2 collective-permute-done.2
  367.8 2.3 bitcast_dynamic-update-slice_fusion.37
  372.5 3.6 collective-permute-start.3
  379.1 2.3 bitcast_dynamic-update-slice_fusion.35
  385.3 3.2 collective-permute-done.2
  391.6 2.3 bitcast_dynamic-update-slice_fusion.37
  396.3 3.6 collective-permute-start.3
  403.0 2.3 bitcast_dynamic-update-slice_fusion.35
  409.2 3.2 collective-permute-done.2
  415.5 2.3 bitcast_dynamic-update-slice_fusion.37
  420.2 3.6 collective-permute-start.3
  433.0 3.2 collective-permute-done.2
  439.4 2.3 bitcast_dynamic-update-slice_fusion.37
  444.0 3.6 collective-permute-start.3
  456.9 3.2 collective-permute-done.2
  463.2 2.3 bitcast_dynamic-update-slice_fusion.37
  467.9 3.9 collective-permute-start.3
  481.1 3.2 collective-permute-done.2
  484.3 2.4 bitcast_convert_fusion
  486.8 2.4 bitcast_convert_fusion.2
  492.5 11.9 %reduce-scatter.17.cloned.1.call-done = bf16[1024,256]{1,0:T(8,128)(2,1)} async-done(((bf16[1024,512]{1,0:T(8,128)(2,1)}), bf16[1024,256]{1,0:T(8,128)(2,1)}) %reduce-scatter.17.cloned.1.call-update) | async-done | bytes 524304 | tf_op jit(solution)/shard_map/reduce_scatter | solution.py:217
  504.4 22.7 %reduce-scatter.13.cloned.1.call-done = bf16[256,1024]{1,0:T(8,128)(2,1)} async-done(((bf16[512,1024]{1,0:T(8,128)(2,1)}), bf16[256,1024]{1,0:T(8,128)(2,1)}) %reduce-scatter.13.cloned.1.call-update) | async-done | bytes 524304 | tf_op jit(solution)/shard_map/reduce_scatter | solution.py:216
  527.1 2.3 bitcast_convert_fusion.3
  531.5 12.7 %collective-permute-done.10 = bf16[1024,256]{1,0:T(8,128)(2,1)S(1)} collective-permute-done((bf16[1024,256]{1,0:T(8,128)(2,1)S(1)}, bf16[1024,256]{1,0:T(8,128)(2,1)S(1)}, u32[]{:S(2)}, u32[]{:S(2)}) %collective-permute-start.10) | collective-permute-done | bytes 524320 | tf_op jit(solution)/shard_map/ppermute | solution.py:23
  545.7 9.4 %collective-permute-done.5 = bf16[256,1024]{1,0:T(8,128)(2,1)S(1)} collective-permute-done((bf16[256,1024]{1,0:T(8,128)(2,1)S(1)}, bf16[256,1024]{1,0:T(8,128)(2,1)S(1)}, u32[]{:S(2)}, u32[]{:S(2)}) %collective-permute-start.5) | collective-permute-done | bytes 524320 | tf_op jit(solution)/shard_map/ppermute | solution.py:23
  557.4 2.4 collective-permute-start.12
  566.8 12.9 %collective-permute-done.16 = bf16[2,128]{1,0:T(2,128)(2,1)S(1)} collective-permute-done((bf16[2,128]{1,0:T(2,128)(2,1)S(1)}, bf16[2,128]{1,0:T(2,128)(2,1)S(1)}, u32[]{:S(2)}, u32[]{:S(2)}) %collective-permute-start.16) | collective-permute-done | bytes 544 | tf_op jit(solution)/shard_map/ppermute | solution.py:23
  579.7 2.6 collective-permute-start.17
  586.0 10.7 %reduce-scatter.11.cloned.1.call-done = bf16[256,1024]{1,0:T(8,128)(2,1)} async-done(((bf16[512,1024]{1,0:T(8,128)(2,1)}), bf16[256,1024]{1,0:T(8,128)(2,1)}) %reduce-scatter.11.cloned.1.call-update) | async-done | bytes 524304 | tf_op jit(solution)/shard_map/reduce_scatter | solution.py:213
  596.7 10.1 %collective-permute-done.7 = bf16[256,1024]{1,0:T(8,128)(2,1)S(1)} collective-permute-done((bf16[256,1024]{1,0:T(8,128)(2,1)S(1)}, bf16[256,1024]{1,0:T(8,128)(2,1)S(1)}, u32[]{:S(2)}, u32[]{:S(2)}) %collective-permute-start.7) | collective-permute-done | bytes 524320 | tf_op jit(solution)/shard_map/ppermute | solution.py:23
  (825 shorter events, 316.5 us)
Async XLA Ops:
  7.2 497.2 %reduce-scatter.17.cloned.1.call-start = ((), (), s32[]{:S(2)}) async-start(), calls=%async_computation.9 | async-start | bytes 1572864 | tf_op jit(solution)/shard_map/reduce_scatter | solution.py:217
  17.5 13.5 %collective-permute-start.1 = (bf16[32,512]{1,0:T(8,128)(2,1)S(1)}, bf16[32,512]{1,0:T(8,128)(2,1)S(1)}, u32[]{:S(2)}, u32[]{:S(2)}) collective-permute-start(bf16[32,512]{1,0:T(8,128)(2,1)S(1)} %get-tuple-element.1341), channel_id=1, source_target_pairs={{2,0},{3,1},{4,2},{5,3},{6,4},{7,5},{8,6},{9,7},{10,8},{11,9},{12,... | collective-permute-start | bytes 98312 | tf_op jit(solution)/shard_map/while/body/eval_jaxpr/ppermute | solution.py:19
  20.8 10.2 %collective-permute-start = (bf16[32,512]{1,0:T(8,128)(2,1)S(1)}, bf16[32,512]{1,0:T(8,128)(2,1)S(1)}, u32[]{:S(2)}, u32[]{:S(2)}) collective-permute-start(bf16[32,512]{1,0:T(8,128)(2,1)S(1)} %get-tuple-element.1337), channel_id=1, source_target_pairs={{0,2},{1,3},{2,4},{3,5},{4,6},{5,7},{6,8},{7,9},{8,10},{9,11},{10,... | collective-permute-start | bytes 98312 | tf_op jit(solution)/shard_map/while/body/eval_jaxpr/ppermute | solution.py:19
  35.6 13.4 %collective-permute-start.1 = (bf16[32,512]{1,0:T(8,128)(2,1)S(1)}, bf16[32,512]{1,0:T(8,128)(2,1)S(1)}, u32[]{:S(2)}, u32[]{:S(2)}) collective-permute-start(bf16[32,512]{1,0:T(8,128)(2,1)S(1)} %get-tuple-element.1341), channel_id=1, source_target_pairs={{2,0},{3,1},{4,2},{5,3},{6,4},{7,5},{8,6},{9,7},{10,8},{11,9},{12,... | collective-permute-start | bytes 98312 | tf_op jit(solution)/shard_map/while/body/eval_jaxpr/ppermute | solution.py:19
  38.8 10.2 %collective-permute-start = (bf16[32,512]{1,0:T(8,128)(2,1)S(1)}, bf16[32,512]{1,0:T(8,128)(2,1)S(1)}, u32[]{:S(2)}, u32[]{:S(2)}) collective-permute-start(bf16[32,512]{1,0:T(8,128)(2,1)S(1)} %get-tuple-element.1337), channel_id=1, source_target_pairs={{0,2},{1,3},{2,4},{3,5},{4,6},{5,7},{6,8},{7,9},{8,10},{9,11},{10,... | collective-permute-start | bytes 98312 | tf_op jit(solution)/shard_map/while/body/eval_jaxpr/ppermute | solution.py:19
  53.6 13.4 %collective-permute-start.1 = (bf16[32,512]{1,0:T(8,128)(2,1)S(1)}, bf16[32,512]{1,0:T(8,128)(2,1)S(1)}, u32[]{:S(2)}, u32[]{:S(2)}) collective-permute-start(bf16[32,512]{1,0:T(8,128)(2,1)S(1)} %get-tuple-element.1341), channel_id=1, source_target_pairs={{2,0},{3,1},{4,2},{5,3},{6,4},{7,5},{8,6},{9,7},{10,8},{11,9},{12,... | collective-permute-start | bytes 98312 | tf_op jit(solution)/shard_map/while/body/eval_jaxpr/ppermute | solution.py:19
  56.8 10.1 %collective-permute-start = (bf16[32,512]{1,0:T(8,128)(2,1)S(1)}, bf16[32,512]{1,0:T(8,128)(2,1)S(1)}, u32[]{:S(2)}, u32[]{:S(2)}) collective-permute-start(bf16[32,512]{1,0:T(8,128)(2,1)S(1)} %get-tuple-element.1337), channel_id=1, source_target_pairs={{0,2},{1,3},{2,4},{3,5},{4,6},{5,7},{6,8},{7,9},{8,10},{9,11},{10,... | collective-permute-start | bytes 98312 | tf_op jit(solution)/shard_map/while/body/eval_jaxpr/ppermute | solution.py:19
  71.6 13.4 %collective-permute-start.1 = (bf16[32,512]{1,0:T(8,128)(2,1)S(1)}, bf16[32,512]{1,0:T(8,128)(2,1)S(1)}, u32[]{:S(2)}, u32[]{:S(2)}) collective-permute-start(bf16[32,512]{1,0:T(8,128)(2,1)S(1)} %get-tuple-element.1341), channel_id=1, source_target_pairs={{2,0},{3,1},{4,2},{5,3},{6,4},{7,5},{8,6},{9,7},{10,8},{11,9},{12,... | collective-permute-start | bytes 98312 | tf_op jit(solution)/shard_map/while/body/eval_jaxpr/ppermute | solution.py:19
  74.8 10.2 %collective-permute-start = (bf16[32,512]{1,0:T(8,128)(2,1)S(1)}, bf16[32,512]{1,0:T(8,128)(2,1)S(1)}, u32[]{:S(2)}, u32[]{:S(2)}) collective-permute-start(bf16[32,512]{1,0:T(8,128)(2,1)S(1)} %get-tuple-element.1337), channel_id=1, source_target_pairs={{0,2},{1,3},{2,4},{3,5},{4,6},{5,7},{6,8},{7,9},{8,10},{9,11},{10,... | collective-permute-start | bytes 98312 | tf_op jit(solution)/shard_map/while/body/eval_jaxpr/ppermute | solution.py:19
  89.6 13.4 %collective-permute-start.1 = (bf16[32,512]{1,0:T(8,128)(2,1)S(1)}, bf16[32,512]{1,0:T(8,128)(2,1)S(1)}, u32[]{:S(2)}, u32[]{:S(2)}) collective-permute-start(bf16[32,512]{1,0:T(8,128)(2,1)S(1)} %get-tuple-element.1341), channel_id=1, source_target_pairs={{2,0},{3,1},{4,2},{5,3},{6,4},{7,5},{8,6},{9,7},{10,8},{11,9},{12,... | collective-permute-start | bytes 98312 | tf_op jit(solution)/shard_map/while/body/eval_jaxpr/ppermute | solution.py:19
  92.9 10.1 %collective-permute-start = (bf16[32,512]{1,0:T(8,128)(2,1)S(1)}, bf16[32,512]{1,0:T(8,128)(2,1)S(1)}, u32[]{:S(2)}, u32[]{:S(2)}) collective-permute-start(bf16[32,512]{1,0:T(8,128)(2,1)S(1)} %get-tuple-element.1337), channel_id=1, source_target_pairs={{0,2},{1,3},{2,4},{3,5},{4,6},{5,7},{6,8},{7,9},{8,10},{9,11},{10,... | collective-permute-start | bytes 98312 | tf_op jit(solution)/shard_map/while/body/eval_jaxpr/ppermute | solution.py:19
  107.6 13.4 %collective-permute-start.1 = (bf16[32,512]{1,0:T(8,128)(2,1)S(1)}, bf16[32,512]{1,0:T(8,128)(2,1)S(1)}, u32[]{:S(2)}, u32[]{:S(2)}) collective-permute-start(bf16[32,512]{1,0:T(8,128)(2,1)S(1)} %get-tuple-element.1341), channel_id=1, source_target_pairs={{2,0},{3,1},{4,2},{5,3},{6,4},{7,5},{8,6},{9,7},{10,8},{11,9},{12,... | collective-permute-start | bytes 98312 | tf_op jit(solution)/shard_map/while/body/eval_jaxpr/ppermute | solution.py:19
  110.9 10.1 %collective-permute-start = (bf16[32,512]{1,0:T(8,128)(2,1)S(1)}, bf16[32,512]{1,0:T(8,128)(2,1)S(1)}, u32[]{:S(2)}, u32[]{:S(2)}) collective-permute-start(bf16[32,512]{1,0:T(8,128)(2,1)S(1)} %get-tuple-element.1337), channel_id=1, source_target_pairs={{0,2},{1,3},{2,4},{3,5},{4,6},{5,7},{6,8},{7,9},{8,10},{9,11},{10,... | collective-permute-start | bytes 98312 | tf_op jit(solution)/shard_map/while/body/eval_jaxpr/ppermute | solution.py:19
  125.6 13.4 %collective-permute-start.1 = (bf16[32,512]{1,0:T(8,128)(2,1)S(1)}, bf16[32,512]{1,0:T(8,128)(2,1)S(1)}, u32[]{:S(2)}, u32[]{:S(2)}) collective-permute-start(bf16[32,512]{1,0:T(8,128)(2,1)S(1)} %get-tuple-element.1341), channel_id=1, source_target_pairs={{2,0},{3,1},{4,2},{5,3},{6,4},{7,5},{8,6},{9,7},{10,8},{11,9},{12,... | collective-permute-start | bytes 98312 | tf_op jit(solution)/shard_map/while/body/eval_jaxpr/ppermute | solution.py:19
  128.9 10.1 %collective-permute-start = (bf16[32,512]{1,0:T(8,128)(2,1)S(1)}, bf16[32,512]{1,0:T(8,128)(2,1)S(1)}, u32[]{:S(2)}, u32[]{:S(2)}) collective-permute-start(bf16[32,512]{1,0:T(8,128)(2,1)S(1)} %get-tuple-element.1337), channel_id=1, source_target_pairs={{0,2},{1,3},{2,4},{3,5},{4,6},{5,7},{6,8},{7,9},{8,10},{9,11},{10,... | collective-permute-start | bytes 98312 | tf_op jit(solution)/shard_map/while/body/eval_jaxpr/ppermute | solution.py:19
  143.6 13.4 %collective-permute-start.1 = (bf16[32,512]{1,0:T(8,128)(2,1)S(1)}, bf16[32,512]{1,0:T(8,128)(2,1)S(1)}, u32[]{:S(2)}, u32[]{:S(2)}) collective-permute-start(bf16[32,512]{1,0:T(8,128)(2,1)S(1)} %get-tuple-element.1341), channel_id=1, source_target_pairs={{2,0},{3,1},{4,2},{5,3},{6,4},{7,5},{8,6},{9,7},{10,8},{11,9},{12,... | collective-permute-start | bytes 98312 | tf_op jit(solution)/shard_map/while/body/eval_jaxpr/ppermute | solution.py:19
  146.9 10.1 %collective-permute-start = (bf16[32,512]{1,0:T(8,128)(2,1)S(1)}, bf16[32,512]{1,0:T(8,128)(2,1)S(1)}, u32[]{:S(2)}, u32[]{:S(2)}) collective-permute-start(bf16[32,512]{1,0:T(8,128)(2,1)S(1)} %get-tuple-element.1337), channel_id=1, source_target_pairs={{0,2},{1,3},{2,4},{3,5},{4,6},{5,7},{6,8},{7,9},{8,10},{9,11},{10,... | collective-permute-start | bytes 98312 | tf_op jit(solution)/shard_map/while/body/eval_jaxpr/ppermute | solution.py:19
  161.6 13.4 %collective-permute-start.1 = (bf16[32,512]{1,0:T(8,128)(2,1)S(1)}, bf16[32,512]{1,0:T(8,128)(2,1)S(1)}, u32[]{:S(2)}, u32[]{:S(2)}) collective-permute-start(bf16[32,512]{1,0:T(8,128)(2,1)S(1)} %get-tuple-element.1341), channel_id=1, source_target_pairs={{2,0},{3,1},{4,2},{5,3},{6,4},{7,5},{8,6},{9,7},{10,8},{11,9},{12,... | collective-permute-start | bytes 98312 | tf_op jit(solution)/shard_map/while/body/eval_jaxpr/ppermute | solution.py:19
  164.9 10.1 %collective-permute-start = (bf16[32,512]{1,0:T(8,128)(2,1)S(1)}, bf16[32,512]{1,0:T(8,128)(2,1)S(1)}, u32[]{:S(2)}, u32[]{:S(2)}) collective-permute-start(bf16[32,512]{1,0:T(8,128)(2,1)S(1)} %get-tuple-element.1337), channel_id=1, source_target_pairs={{0,2},{1,3},{2,4},{3,5},{4,6},{5,7},{6,8},{7,9},{8,10},{9,11},{10,... | collective-permute-start | bytes 98312 | tf_op jit(solution)/shard_map/while/body/eval_jaxpr/ppermute | solution.py:19
  179.6 13.4 %collective-permute-start.1 = (bf16[32,512]{1,0:T(8,128)(2,1)S(1)}, bf16[32,512]{1,0:T(8,128)(2,1)S(1)}, u32[]{:S(2)}, u32[]{:S(2)}) collective-permute-start(bf16[32,512]{1,0:T(8,128)(2,1)S(1)} %get-tuple-element.1341), channel_id=1, source_target_pairs={{2,0},{3,1},{4,2},{5,3},{6,4},{7,5},{8,6},{9,7},{10,8},{11,9},{12,... | collective-permute-start | bytes 98312 | tf_op jit(solution)/shard_map/while/body/eval_jaxpr/ppermute | solution.py:19
  182.9 10.1 %collective-permute-start = (bf16[32,512]{1,0:T(8,128)(2,1)S(1)}, bf16[32,512]{1,0:T(8,128)(2,1)S(1)}, u32[]{:S(2)}, u32[]{:S(2)}) collective-permute-start(bf16[32,512]{1,0:T(8,128)(2,1)S(1)} %get-tuple-element.1337), channel_id=1, source_target_pairs={{0,2},{1,3},{2,4},{3,5},{4,6},{5,7},{6,8},{7,9},{8,10},{9,11},{10,... | collective-permute-start | bytes 98312 | tf_op jit(solution)/shard_map/while/body/eval_jaxpr/ppermute | solution.py:19
  197.6 13.4 %collective-permute-start.1 = (bf16[32,512]{1,0:T(8,128)(2,1)S(1)}, bf16[32,512]{1,0:T(8,128)(2,1)S(1)}, u32[]{:S(2)}, u32[]{:S(2)}) collective-permute-start(bf16[32,512]{1,0:T(8,128)(2,1)S(1)} %get-tuple-element.1341), channel_id=1, source_target_pairs={{2,0},{3,1},{4,2},{5,3},{6,4},{7,5},{8,6},{9,7},{10,8},{11,9},{12,... | collective-permute-start | bytes 98312 | tf_op jit(solution)/shard_map/while/body/eval_jaxpr/ppermute | solution.py:19
  200.9 10.1 %collective-permute-start = (bf16[32,512]{1,0:T(8,128)(2,1)S(1)}, bf16[32,512]{1,0:T(8,128)(2,1)S(1)}, u32[]{:S(2)}, u32[]{:S(2)}) collective-permute-start(bf16[32,512]{1,0:T(8,128)(2,1)S(1)} %get-tuple-element.1337), channel_id=1, source_target_pairs={{0,2},{1,3},{2,4},{3,5},{4,6},{5,7},{6,8},{7,9},{8,10},{9,11},{10,... | collective-permute-start | bytes 98312 | tf_op jit(solution)/shard_map/while/body/eval_jaxpr/ppermute | solution.py:19
  222.3 14.8 %collective-permute-start.3 = (bf16[32,512]{1,0:T(8,128)(2,1)}, bf16[32,512]{1,0:T(8,128)(2,1)}, u32[]{:S(2)}, u32[]{:S(2)}) collective-permute-start(bf16[32,512]{1,0:T(8,128)(2,1)} %fusion.139), channel_id=1, source_target_pairs={{0,2},{1,3},{2,4},{3,5},{4,6},{5,7},{6,8},{7,9},{8,10},{9,11},{10,... | collective-permute-start | bytes 98312 | tf_op jit(solution)/shard_map/while/body/eval_jaxpr/ppermute | solution.py:19
  235.1 5.8 collective-permute-start.2
  248.7 13.0 %collective-permute-start.3 = (bf16[32,512]{1,0:T(8,128)(2,1)}, bf16[32,512]{1,0:T(8,128)(2,1)}, u32[]{:S(2)}, u32[]{:S(2)}) collective-permute-start(bf16[32,512]{1,0:T(8,128)(2,1)} %fusion.139), channel_id=1, source_target_pairs={{0,2},{1,3},{2,4},{3,5},{4,6},{5,7},{6,8},{7,9},{8,10},{9,11},{10,... | collective-permute-start | bytes 98312 | tf_op jit(solution)/shard_map/while/body/eval_jaxpr/ppermute | solution.py:19
  259.2 5.8 collective-permute-start.2
  272.8 14.8 %collective-permute-start.3 = (bf16[32,512]{1,0:T(8,128)(2,1)}, bf16[32,512]{1,0:T(8,128)(2,1)}, u32[]{:S(2)}, u32[]{:S(2)}) collective-permute-start(bf16[32,512]{1,0:T(8,128)(2,1)} %fusion.139), channel_id=1, source_target_pairs={{0,2},{1,3},{2,4},{3,5},{4,6},{5,7},{6,8},{7,9},{8,10},{9,11},{10,... | collective-permute-start | bytes 98312 | tf_op jit(solution)/shard_map/while/body/eval_jaxpr/ppermute | solution.py:19
  285.0 5.8 collective-permute-start.2
  298.6 13.0 %collective-permute-start.3 = (bf16[32,512]{1,0:T(8,128)(2,1)}, bf16[32,512]{1,0:T(8,128)(2,1)}, u32[]{:S(2)}, u32[]{:S(2)}) collective-permute-start(bf16[32,512]{1,0:T(8,128)(2,1)} %fusion.139), channel_id=1, source_target_pairs={{0,2},{1,3},{2,4},{3,5},{4,6},{5,7},{6,8},{7,9},{8,10},{9,11},{10,... | collective-permute-start | bytes 98312 | tf_op jit(solution)/shard_map/while/body/eval_jaxpr/ppermute | solution.py:19
  309.0 5.8 collective-permute-start.2
  322.6 14.8 %collective-permute-start.3 = (bf16[32,512]{1,0:T(8,128)(2,1)}, bf16[32,512]{1,0:T(8,128)(2,1)}, u32[]{:S(2)}, u32[]{:S(2)}) collective-permute-start(bf16[32,512]{1,0:T(8,128)(2,1)} %fusion.139), channel_id=1, source_target_pairs={{0,2},{1,3},{2,4},{3,5},{4,6},{5,7},{6,8},{7,9},{8,10},{9,11},{10,... | collective-permute-start | bytes 98312 | tf_op jit(solution)/shard_map/while/body/eval_jaxpr/ppermute | solution.py:19
  334.9 5.8 collective-permute-start.2
  348.5 13.0 %collective-permute-start.3 = (bf16[32,512]{1,0:T(8,128)(2,1)}, bf16[32,512]{1,0:T(8,128)(2,1)}, u32[]{:S(2)}, u32[]{:S(2)}) collective-permute-start(bf16[32,512]{1,0:T(8,128)(2,1)} %fusion.139), channel_id=1, source_target_pairs={{0,2},{1,3},{2,4},{3,5},{4,6},{5,7},{6,8},{7,9},{8,10},{9,11},{10,... | collective-permute-start | bytes 98312 | tf_op jit(solution)/shard_map/while/body/eval_jaxpr/ppermute | solution.py:19
  358.8 5.8 collective-permute-start.2
  372.5 12.8 %collective-permute-start.3 = (bf16[32,512]{1,0:T(8,128)(2,1)}, bf16[32,512]{1,0:T(8,128)(2,1)}, u32[]{:S(2)}, u32[]{:S(2)}) collective-permute-start(bf16[32,512]{1,0:T(8,128)(2,1)} %fusion.139), channel_id=1, source_target_pairs={{0,2},{1,3},{2,4},{3,5},{4,6},{5,7},{6,8},{7,9},{8,10},{9,11},{10,... | collective-permute-start | bytes 98312 | tf_op jit(solution)/shard_map/while/body/eval_jaxpr/ppermute | solution.py:19
  382.7 5.8 collective-permute-start.2
  396.3 12.9 %collective-permute-start.3 = (bf16[32,512]{1,0:T(8,128)(2,1)}, bf16[32,512]{1,0:T(8,128)(2,1)}, u32[]{:S(2)}, u32[]{:S(2)}) collective-permute-start(bf16[32,512]{1,0:T(8,128)(2,1)} %fusion.139), channel_id=1, source_target_pairs={{0,2},{1,3},{2,4},{3,5},{4,6},{5,7},{6,8},{7,9},{8,10},{9,11},{10,... | collective-permute-start | bytes 98312 | tf_op jit(solution)/shard_map/while/body/eval_jaxpr/ppermute | solution.py:19
  406.6 5.8 collective-permute-start.2
  420.2 12.8 %collective-permute-start.3 = (bf16[32,512]{1,0:T(8,128)(2,1)}, bf16[32,512]{1,0:T(8,128)(2,1)}, u32[]{:S(2)}, u32[]{:S(2)}) collective-permute-start(bf16[32,512]{1,0:T(8,128)(2,1)} %fusion.139), channel_id=1, source_target_pairs={{0,2},{1,3},{2,4},{3,5},{4,6},{5,7},{6,8},{7,9},{8,10},{9,11},{10,... | collective-permute-start | bytes 98312 | tf_op jit(solution)/shard_map/while/body/eval_jaxpr/ppermute | solution.py:19
  430.4 5.8 collective-permute-start.2
  444.0 12.8 %collective-permute-start.3 = (bf16[32,512]{1,0:T(8,128)(2,1)}, bf16[32,512]{1,0:T(8,128)(2,1)}, u32[]{:S(2)}, u32[]{:S(2)}) collective-permute-start(bf16[32,512]{1,0:T(8,128)(2,1)} %fusion.139), channel_id=1, source_target_pairs={{0,2},{1,3},{2,4},{3,5},{4,6},{5,7},{6,8},{7,9},{8,10},{9,11},{10,... | collective-permute-start | bytes 98312 | tf_op jit(solution)/shard_map/while/body/eval_jaxpr/ppermute | solution.py:19
  454.3 5.8 collective-permute-start.2
  467.9 13.2 %collective-permute-start.3 = (bf16[32,512]{1,0:T(8,128)(2,1)}, bf16[32,512]{1,0:T(8,128)(2,1)}, u32[]{:S(2)}, u32[]{:S(2)}) collective-permute-start(bf16[32,512]{1,0:T(8,128)(2,1)} %fusion.139), channel_id=1, source_target_pairs={{0,2},{1,3},{2,4},{3,5},{4,6},{5,7},{6,8},{7,9},{8,10},{9,11},{10,... | collective-permute-start | bytes 98312 | tf_op jit(solution)/shard_map/while/body/eval_jaxpr/ppermute | solution.py:19
  478.5 5.8 collective-permute-start.2
  486.7 40.4 %reduce-scatter.13.cloned.1.call-start = ((), (), s32[]{:S(2)}) async-start(), calls=%async_computation.7 | async-start | bytes 1572864 | tf_op jit(solution)/shard_map/reduce_scatter | solution.py:216
  489.2 70.6 %reduce-scatter.21.cloned.1.call-start = ((), (), s32[]{:S(2)}) async-start(), calls=%async_computation.11 | async-start | bytes 98304
  490.1 92.3 %reduce-scatter.19.cloned.1.call-start = ((), (), s32[]{:S(2)}) async-start(), calls=%async_computation.10 | async-start | bytes 98304
  490.9 93.3 %reduce-scatter.15.cloned.1.call-start = ((), (), s32[]{:S(2)}) async-start(), calls=%async_computation.8 | async-start | bytes 1572864 | tf_op jit(solution)/shard_map/reduce_scatter | solution.py:214
  492.5 104.2 %reduce-scatter.11.cloned.1.call-start = ((), (), s32[]{:S(2)}) async-start(), calls=%async_computation.6 | async-start | bytes 1572864 | tf_op jit(solution)/shard_map/reduce_scatter | solution.py:213
  504.4 25.0 %collective-permute-start.9 = (bf16[1024,256]{1,0:T(8,128)(2,1)}, bf16[1024,256]{1,0:T(8,128)(2,1)S(1)}, u32[]{:S(2)}, u32[]{:S(2)}) collective-permute-start(bf16[1024,256]{1,0:T(8,128)(2,1)} %reduce-scatter.17.cloned.1.call-done), channel_id=1, source_target_pairs={{0,1},{1,0},{2,3},{3,2},{4,5},{5,4},{6,7},{7,6},{8,9},{9,8},{10,11... | collective-permute-start | bytes 1572872 | tf_op jit(solution)/shard_map/ppermute | solution.py:23
  527.1 3.9 collective-permute-start.4
  529.4 14.8 %collective-permute-start.10 = (bf16[1024,256]{1,0:T(8,128)(2,1)S(1)}, bf16[1024,256]{1,0:T(8,128)(2,1)S(1)}, u32[]{:S(2)}, u32[]{:S(2)}) collective-permute-start(bf16[1024,256]{1,0:T(8,128)(2,1)S(1)} %collective-permute-done.9), channel_id=1, source_target_pairs={{0,2},{1,3},{2,0},{3,1},{4,6},{5,7},{6,4},{7,5},{8,10},{9,11},{10,... | collective-permute-start | bytes 1572872 | tf_op jit(solution)/shard_map/ppermute | solution.py:23
  531.0 24.1 %collective-permute-start.5 = (bf16[256,1024]{1,0:T(8,128)(2,1)S(1)}, bf16[256,1024]{1,0:T(8,128)(2,1)S(1)}, u32[]{:S(2)}, u32[]{:S(2)}) collective-permute-start(bf16[256,1024]{1,0:T(8,128)(2,1)S(1)} %collective-permute-done.4), channel_id=1, source_target_pairs={{0,2},{1,3},{2,0},{3,1},{4,6},{5,7},{6,4},{7,5},{8,10},{9,11},{10,... | collective-permute-start | bytes 1572872 | tf_op jit(solution)/shard_map/ppermute | solution.py:23
  544.2 13.2 %collective-permute-start.11 = (bf16[1024,256]{1,0:T(8,128)(2,1)S(1)}, bf16[1024,256]{1,0:T(8,128)(2,1)S(1)}, u32[]{:S(2)}, u32[]{:S(2)}) collective-permute-start(bf16[1024,256]{1,0:T(8,128)(2,1)S(1)} %collective-permute-done.10), channel_id=1, source_target_pairs={{0,4},{1,5},{2,6},{3,7},{4,0},{5,1},{6,2},{7,3},{8,12},{9,13},{10,... | collective-permute-start | bytes 1572872 | tf_op jit(solution)/shard_map/ppermute | solution.py:23
  555.1 28.1 %collective-permute-start.6 = (bf16[256,1024]{1,0:T(8,128)(2,1)S(1)}, bf16[256,1024]{1,0:T(8,128)(2,1)S(1)}, u32[]{:S(2)}, u32[]{:S(2)}) collective-permute-start(bf16[256,1024]{1,0:T(8,128)(2,1)S(1)} %collective-permute-done.5), channel_id=1, source_target_pairs={{0,4},{1,5},{2,6},{3,7},{4,0},{5,1},{6,2},{7,3},{8,12},{9,13},{10,... | collective-permute-start | bytes 1572872 | tf_op jit(solution)/shard_map/ppermute | solution.py:23
  557.4 26.9 %collective-permute-start.12 = (bf16[1024,256]{1,0:T(8,128)(2,1)S(1)}, bf16[1024,256]{1,0:T(8,128)(2,1)S(1)}, u32[]{:S(2)}, u32[]{:S(2)}) collective-permute-start(bf16[1024,256]{1,0:T(8,128)(2,1)S(1)} %collective-permute-done.11), channel_id=1, source_target_pairs={{0,8},{1,9},{2,10},{3,11},{4,12},{5,13},{6,14},{7,15},{8,0},{9,1},... | collective-permute-start | bytes 1572872 | tf_op jit(solution)/shard_map/ppermute | solution.py:23
  561.8 3.5 collective-permute-start.15
  565.3 14.4 %collective-permute-start.16 = (bf16[2,128]{1,0:T(2,128)(2,1)S(1)}, bf16[2,128]{1,0:T(2,128)(2,1)S(1)}, u32[]{:S(2)}, u32[]{:S(2)}) collective-permute-start(bf16[2,128]{1,0:T(2,128)(2,1)S(1)} %collective-permute-done.15), channel_id=1, source_target_pairs={{0,4},{1,5},{2,6},{3,7},{4,0},{5,1},{6,2},{7,3},{8,12},{9,13},{10,... | collective-permute-start | bytes 1544 | tf_op jit(solution)/shard_map/ppermute | solution.py:23
  579.7 4.4 collective-permute-start.17
  583.1 23.6 %collective-permute-start.7 = (bf16[256,1024]{1,0:T(8,128)(2,1)S(1)}, bf16[256,1024]{1,0:T(8,128)(2,1)S(1)}, u32[]{:S(2)}, u32[]{:S(2)}) collective-permute-start(bf16[256,1024]{1,0:T(8,128)(2,1)S(1)} %collective-permute-done.6), channel_id=1, source_target_pairs={{0,8},{1,9},{2,10},{3,11},{4,12},{5,13},{6,14},{7,15},{8,0},{9,1},... | collective-permute-start | bytes 1572872 | tf_op jit(solution)/shard_map/ppermute | solution.py:23
  584.2 24.0 %collective-permute-start.18 = (bf16[1,128]{1,0:T(2,128)(2,1)S(1)}, bf16[1,128]{1,0:T(2,128)(2,1)S(1)}, u32[]{:S(2)}, u32[]{:S(2)}) collective-permute-start(bf16[1,128]{1,0:T(2,128)(2,1)S(1)} %fusion.95), channel_id=1, source_target_pairs={{0,1},{1,0},{2,3},{3,2},{4,5},{5,4},{6,7},{7,6},{8,9},{9,8},{10,11... | collective-permute-start | bytes 776 | tf_op jit(solution)/shard_map/ppermute | solution.py:23
  585.5 23.2 %collective-permute-start.13 = (bf16[512,256]{1,0:T(8,128)(2,1)S(1)}, bf16[512,256]{1,0:T(8,128)(2,1)S(1)}, u32[]{:S(2)}, u32[]{:S(2)}) collective-permute-start(bf16[512,256]{1,0:T(8,128)(2,1)S(1)} %dynamic-slice_convert_fusion), channel_id=1, source_target_pairs={{0,1},{1,0},{2,3},{3,2},{4,5},{5,4},{6,7},{7,6},{8,9},{9,8},{10,11... | collective-permute-start | bytes 786440 | tf_op jit(solution)/shard_map/ppermute | solution.py:23
  608.0 1.6 collective-permute-start.8
  (75 other events, 560.3 us)
Sparse Core Ops, SparseCore 0:
  486.8 17.5 reduce-scatter.16
  506.7 20.3 reduce-scatter.12
  529.8 9.8 reduce-scatter.20
  541.8 9.8 reduce-scatter.18
  553.8 20.3 reduce-scatter.14
  576.4 20.3 reduce-scatter.10
where the time goes:
time: 627 us; the launch traced here: 617 us
  starting transfers between devices  150 us (24%)
  waiting for transfers between devices  131 us (21%)
  matrix products  124 us (20%)
  other arithmetic  101 us (16%)
  local copies, waits for them, and re-layouts  94.2 us (15%)
  between operations  14.4 us (2%)
    ppermute x44, starting transfers between devices, passed_along(): return lax.ppermute(block, axis, route)  135 us
    dynamic_slice x154, local copies, waits for them, and re-layouts, put_slot(): previous = lax.dynamic_index_in_dim(stack, slot, 0, keepdims=False)  81.5 us
    dot_general x22, matrix products, backward_tick(): lax.dot_general(incoming, down_weight[role], (((1,), (1,)), ((), ())), pr...  49.9 us
    ppermute x15, waiting for transfers between devices, partner(): lax.ppermute(shard, axis, [(i, i ^ 1 << stride) for i in range(lax.axis_s...  49.8 us
    dynamic_update_slice x66, other arithmetic, put_slot(): return lax.dynamic_update_index_in_dim(stack, chosen, slot, 0)  48.8 us
    ppermute x44, waiting for transfers between devices, passed_along(): return lax.ppermute(block, axis, route)  36.1 us
    dot_general x22, matrix products, backward_tick(): lax.dot_general(pre_grad, up_weight[role], (((1,), (1,)), ((), ())), pref...  32 us
    reduce_scatter x1, waiting for transfers between devices, body(): lax.psum_scatter(partials[3], 'dp', scatter_dimension=0, tiled=True)  22.7 us
  transfers between devices with their start and end apart: 65, of which 23 were waited for; matrix products, arithmetic and copies ran while one was open for 28% of the time, Pallas kernels for 0%

commit v1 on v0

v1 whole, which is shorter than its diff:
```python
import functools
import math

import jax
import jax.numpy as jnp
from jax import lax
from jax.experimental import pallas as pl
from jax.experimental.pallas import tpu as pltpu
from jax.sharding import PartitionSpec as P

GELU_C = 0.7978845608028654
CUBIC = 0.044715
CHUNKS_PER_RELAY = 2
MESH = pl.DeviceIdType.MESH


def dot_nt(left, right):
    return lax.dot_general(left, right, (((1,), (1,)), ((), ())), preferred_element_type=jnp.float32)


def dot_tn(left, right):
    return lax.dot_general(left, right, (((0,), (0,)), ((), ())), preferred_element_type=jnp.float32)


def kernel(
    segments,
    replicas,
    loss_scale,
    rising,
    falling,
    up_hbm,
    down_hbm,
    gain_ref,
    out_up,
    out_down,
    out_gain,
    up,
    down,
    x_in,
    y_out,
    xh_st,
    inv_st,
    n_st,
    p_st,
    a_st,
    t_st,
    dy_in,
    dx_out,
    da_st,
    gain_acc,
    gain_sum,
    gain_core,
    gain_dp,
    cs_up,
    cs_down,
    cr_up,
    cr_down,
    acc_up,
    acc_down,
    st_up,
    st_down,
    dr_up,
    dr_down,
    load_sem,
    feed_sem,
    fs_sem,
    fr_sem,
    bs_sem,
    br_sem,
    cs_sem,
    cr_sem,
    ds_sem,
    dr_sem,
):
    place = lax.axis_index("segment")
    rep = lax.axis_index("dp")
    pair = place // 2
    core = place % 2
    last = segments // 2 - 1
    chunks, rows, width = x_in.shape
    hidden_units = up.shape[1]
    half = hidden_units // 2
    micro = rising.shape[0]
    local_rows = rising.shape[1] // 2
    mates = place + 1 - 2 * core
    slice_d = width // replicas

    load_up = pltpu.make_async_copy(up_hbm.at[0], up, load_sem.at[0])
    load_down = pltpu.make_async_copy(down_hbm.at[0], down, load_sem.at[1])
    load_up.start()
    load_down.start()

    per_chunk = rows // local_rows

    def feed_copy(which, m):
        src = (rising, falling)[which]
        flat = which * micro + m
        return pltpu.make_async_copy(
            src.at[m, pl.ds(pl.multiple_of(core * local_rows, local_rows), local_rows), :],
            x_in.at[flat // per_chunk, pl.ds((flat % per_chunk) * local_rows, local_rows), :],
            feed_sem.at[flat],
        )

    @pl.when(pair == 0)
    def _():
        for which in (0, 1):
            for m in range(micro):
                feed_copy(which, m).start()

    barrier = pltpu.get_barrier_semaphore()

    @pl.when(pair > 0)
    def _():
        pl.semaphore_signal(barrier, inc=1, device_id={"segment": place - 2}, device_id_type=MESH)

    @pl.when(pair < last)
    def _():
        pl.semaphore_signal(barrier, inc=1, device_id={"segment": place + 2}, device_id_type=MESH)

    pl.semaphore_signal(barrier, inc=1, device_id={"segment": mates}, device_id_type=MESH)
    for off in range(1, replicas):
        pl.semaphore_signal(
            barrier, inc=1, device_id={"dp": lax.rem(rep + off, replicas)}, device_id_type=MESH
        )
    gain_acc[...] = jnp.zeros_like(gain_acc)
    load_up.wait()
    load_down.wait()
    pl.semaphore_wait(
        barrier,
        replicas + jnp.where(pair > 0, 1, 0) + jnp.where(pair < last, 1, 0),
    )

    def send_forward(i):
        return pltpu.make_async_remote_copy(
            src_ref=y_out.at[i],
            dst_ref=x_in.at[i],
            send_sem=fs_sem.at[i],
            recv_sem=fr_sem.at[i],
            device_id={"segment": place + 2},
            device_id_type=MESH,
        )

    def send_backward(i):
        return pltpu.make_async_remote_copy(
            src_ref=dx_out.at[i],
            dst_ref=dy_in.at[i],
            send_sem=bs_sem.at[i],
            recv_sem=br_sem.at[i],
            device_id={"segment": place - 2},
            device_id_type=MESH,
        )

    @pl.when(pair == 0)
    def _():
        for which in (0, 1):
            for m in range(micro):
                feed_copy(which, m).wait()

    gain_row = gain_ref[0:1, :]

    def forward(i, carry):
        @pl.when(pair > 0)
        def _():
            send_forward(i).wait_recv()

        x = x_in[i].astype(jnp.float32)
        centre = jnp.mean(x, axis=-1, keepdims=True)
        xc = x - centre
        spread = jnp.mean(xc * xc, axis=-1, keepdims=True)
        inverse = lax.rsqrt(spread + 1e-05)
        xh = xc * inverse
        n = (xh * gain_row).astype(jnp.bfloat16)
        a = jnp.dot(n, up[...], preferred_element_type=jnp.float32)
        t = jnp.tanh(GELU_C * (a + CUBIC * a * a * a))
        p = (0.5 * a * (1.0 + t)).astype(jnp.bfloat16)
        y = (x + jnp.dot(p, down[...], preferred_element_type=jnp.float32)).astype(jnp.bfloat16)

        @pl.when(pair < last)
        def _():
            y_out[i] = y
            send_forward(i).start()

        @pl.when(pair == last)
        def _():
            dy_in[i] = (y.astype(jnp.float32) * loss_scale).astype(jnp.bfloat16)

        xh_st[i] = xh
        inv_st[i] = jnp.broadcast_to(inverse, (rows, 128))
        span = pl.ds(pl.multiple_of(i * rows, rows), rows)
        n_st[span, :] = n
        p_st[span, :] = p
        a_st[i] = 0.5 * (1.0 + t) + 0.5 * a * (1.0 - t * t) * GELU_C * (1.0 + 3.0 * CUBIC * a * a)
        return carry

    lax.fori_loop(0, chunks, forward, 0)

    def backward(i, carry):
        @pl.when(pair < last)
        def _():
            send_backward(i).wait_recv()

        dy = dy_in[i]
        dp = dot_nt(dy, down[...])
        da = (dp * a_st[i]).astype(jnp.bfloat16)
        dn = dot_nt(da, up[...])
        xh = xh_st[i]
        e = dn * gain_row
        m1 = jnp.mean(e, axis=-1, keepdims=True)
        m2 = jnp.mean(e * xh, axis=-1, keepdims=True)
        inverse = inv_st[i][:, 0:1]
        dx = (dy.astype(jnp.float32) + inverse * (e - m1 - xh * m2)).astype(jnp.bfloat16)

        @pl.when(pair > 0)
        def _():
            dx_out[i] = dx
            send_backward(i).start()

        span = pl.ds(pl.multiple_of(i * rows, rows), rows)
        da_st[span, :] = da
        t_st[span, :] = dy
        part = (dn * xh).reshape(rows // 8, 8, width)
        gain_acc[...] += jnp.sum(part, axis=0)
        return carry

    lax.fori_loop(0, chunks, backward, 0)

    mine = pl.ds(pl.multiple_of(core * half, half), half)
    theirs = pl.ds(pl.multiple_of((1 - core) * half, half), half)

    def to_core(src, dst, slot):
        return pltpu.make_async_remote_copy(
            src_ref=src,
            dst_ref=dst,
            send_sem=cs_sem.at[slot],
            recv_sem=cr_sem.at[slot],
            device_id={"segment": mates},
            device_id_type=MESH,
        )

    def to_replica(src, dst, slot, off):
        return pltpu.make_async_remote_copy(
            src_ref=src,
            dst_ref=dst.at[off - 1],
            send_sem=ds_sem.at[slot, off - 1],
            recv_sem=dr_sem.at[slot, off - 1],
            device_id={"dp": lax.rem(rep + off, replicas)},
            device_id_type=MESH,
        )

    def target(off):
        return lax.rem(rep + off, replicas)

    core_gain = to_core(gain_acc, gain_core, 2)
    core_gain.start()
    cs_up[...] = dot_tn(n_st[...], da_st[:, theirs]).astype(jnp.bfloat16)
    core_up = to_core(cs_up, cr_up, 0)
    core_up.start()
    cs_down[...] = dot_tn(p_st[:, theirs], t_st[...]).astype(jnp.bfloat16)
    core_down = to_core(cs_down, cr_down, 1)
    core_down.start()

    core_gain.wait()
    gain_sum[...] = gain_acc[...] + gain_core[...]
    for off in range(1, replicas):
        to_replica(gain_sum, gain_dp, 2, off).start()

    total_up = dot_tn(n_st[...], da_st[:, mine])
    core_up.wait()
    total_up = total_up + cr_up[...].astype(jnp.float32)
    for j in range(replicas):
        block = total_up[j * slice_d : (j + 1) * slice_d, :]
        acc_up[j] = block
        st_up[j] = block.astype(jnp.bfloat16)
    for off in range(1, replicas):
        to_replica(st_up.at[target(off)], dr_up, 0, off).start()

    total_down = dot_tn(p_st[:, mine], t_st[...])
    core_down.wait()
    total_down = total_down + cr_down[...].astype(jnp.float32)
    for j in range(replicas):
        block = total_down[:, j * slice_d : (j + 1) * slice_d]
        acc_down[j] = block
        st_down[j] = block.astype(jnp.bfloat16)
    for off in range(1, replicas):
        to_replica(st_down.at[target(off)], dr_down, 1, off).start()

    @pl.when(pair < last)
    def _():
        for i in range(chunks):
            send_forward(i).wait_send()

    @pl.when(pair > 0)
    def _():
        for i in range(chunks):
            send_backward(i).wait_send()

    gains = gain_sum[...]
    for off in range(1, replicas):
        to_replica(gain_sum, gain_dp, 2, off).wait()
        gains = gains + gain_dp[off - 1]
    gains = jnp.sum(gains, axis=0, keepdims=True)
    wide = out_gain.shape[1]
    for c in (0, 1):
        for j in range(replicas):
            start = c * (width // 2) + j * wide

            @pl.when((core == c) & (rep == j))
            def _():
                out_gain[...] = gains[:, start : start + wide]

    res = acc_up[rep]
    for off in range(1, replicas):
        to_replica(st_up.at[target(off)], dr_up, 0, off).wait()
        res = res + dr_up[off - 1].astype(jnp.float32)
    out_up[...] = res
    res = acc_down[rep]
    for off in range(1, replicas):
        to_replica(st_down.at[target(off)], dr_down, 1, off).wait()
        res = res + dr_down[off - 1].astype(jnp.float32)
    out_down[...] = res


def body(feed_rising, feed_falling, up_weight, down_weight, norm_gain):
    segments = lax.axis_size("segment")
    replicas = lax.axis_size("dp")
    micro, rep_rows, width = feed_rising.shape
    local_rows = rep_rows // 2
    hidden = up_weight.shape[2]
    half = hidden // 2
    loss_scale = 1.0 / math.sqrt(2.0 * micro * rep_rows * replicas)
    chunks = 2 * CHUNKS_PER_RELAY
    rows = 2 * micro * local_rows // chunks
    total = chunks * rows
    slice_d = width // replicas
    bf16, f32 = jnp.bfloat16, jnp.float32
    vmem = pl.BlockSpec(memory_space=pltpu.VMEM)
    anym = pl.BlockSpec(memory_space=pl.ANY)
    others = max(replicas - 1, 1)
    flops = 12 * total * width * hidden
    return pl.pallas_call(
        functools.partial(kernel, segments, replicas, loss_scale),
        out_shape=(
            jax.ShapeDtypeStruct((slice_d, half), f32),
            jax.ShapeDtypeStruct((half, slice_d), f32),
            jax.ShapeDtypeStruct((1, width // 2 // replicas), f32),
        ),
        in_specs=[anym, anym, anym, anym, vmem],
        out_specs=(vmem, vmem, vmem),
        scratch_shapes=[
            pltpu.VMEM((width, hidden), bf16),
            pltpu.VMEM((hidden, width), bf16),
            pltpu.VMEM((chunks, rows, width), bf16),
            pltpu.VMEM((chunks, rows, width), bf16),
            pltpu.VMEM((chunks, rows, width), f32),
            pltpu.VMEM((chunks, rows, 128), f32),
            pltpu.VMEM((total, width), bf16),
            pltpu.VMEM((total, hidden), bf16),
            pltpu.VMEM((chunks, rows, hidden), f32),
            pltpu.VMEM((total, width), bf16),
            pltpu.VMEM((chunks, rows, width), bf16),
            pltpu.VMEM((chunks, rows, width), bf16),
            pltpu.VMEM((total, hidden), bf16),
            pltpu.VMEM((8, width), f32),
            pltpu.VMEM((8, width), f32),
            pltpu.VMEM((8, width), f32),
            pltpu.VMEM((others, 8, width), f32),
            pltpu.VMEM((width, half), bf16),
            pltpu.VMEM((half, width), bf16),
            pltpu.VMEM((width, half), bf16),
            pltpu.VMEM((half, width), bf16),
            pltpu.VMEM((replicas, slice_d, half), f32),
            pltpu.VMEM((replicas, half, slice_d), f32),
            pltpu.VMEM((replicas, slice_d, half), bf16),
            pltpu.VMEM((replicas, half, slice_d), bf16),
            pltpu.VMEM((others, slice_d, half), bf16),
            pltpu.VMEM((others, half, slice_d), bf16),
            pltpu.SemaphoreType.DMA((2,)),
            pltpu.SemaphoreType.DMA((2 * micro,)),
            pltpu.SemaphoreType.DMA((chunks,)),
            pltpu.SemaphoreType.DMA((chunks,)),
            pltpu.SemaphoreType.DMA((chunks,)),
            pltpu.SemaphoreType.DMA((chunks,)),
            pltpu.SemaphoreType.DMA((3,)),
            pltpu.SemaphoreType.DMA((3,)),
            pltpu.SemaphoreType.DMA((3, others)),
            pltpu.SemaphoreType.DMA((3, others)),
        ],
        compiler_params=pltpu.CompilerParams(
            collective_id=0, has_side_effects=True, vmem_limit_bytes=40 * 1024 * 1024
        ),
        cost_estimate=pl.CostEstimate(
            flops=flops, bytes_accessed=6 * 1024 * 1024, transcendentals=total * hidden
        ),
        name="relay",
    )(feed_rising, feed_falling, up_weight, down_weight, norm_gain)


def solution(mesh):
    return jax.shard_map(
        body,
        mesh=mesh,
        in_specs=(
            P(None, "dp", None),
            P(None, "dp", None),
            P("segment", None, None),
            P("segment", None, None),
            P("segment", None),
        ),
        out_specs=(P("dp", "segment"), P("segment", "dp"), P("segment", "dp")),
        check_vma=False,
    )
```

time: 627 us -> 96.6 us (0.15); the launches traced: 617 us -> 96.4 us
  starting transfers between devices: 150 us -> 0 us
  waiting for transfers between devices: 131 us -> 0 us
  matrix products: 124 us -> 0 us
  other arithmetic: 101 us -> 0 us
  Pallas kernels: 0 us -> 87.8 us
  local copies, waits for them, and re-layouts: 94.2 us -> 7.86 us
  between operations: 14.4 us -> 0.65 us
    ppermute x59 -> x0, starting transfers between devices: 149 us -> none  [the longest x44 135 us: passed_along(): return lax.ppermute(block, axis, route)]
    dot_general x92 -> x0, matrix products: 124 us -> none  [the longest x22 49.9 us: backward_tick(): lax.dot_general(incoming, down_weight[role], (((1,), (1,)), ((), ())), pr...]
    pallas_call x0 -> x1, Pallas kernels: none -> 87.8 us  [body(): pl.pallas_call(functools.partial(kernel, segments, replicas, loss_scale),...]
    ppermute x59 -> x0, waiting for transfers between devices: 85.9 us -> none  [the longest x15 49.8 us: partner(): lax.ppermute(shard, axis, [(i, i ^ 1 << stride) for i in range(lax.axis_s...]
    dynamic_slice x155 -> x0, local copies, waits for them, and re-layouts: 83.3 us -> none  [the longest x154 81.5 us: put_slot(): previous = lax.dynamic_index_in_dim(stack, slot, 0, keepdims=False)]
    dynamic_update_slice x66 -> x0, other arithmetic: 48.8 us -> none  [put_slot(): return lax.dynamic_update_index_in_dim(stack, chosen, slot, 0)]
    reduce_scatter x4 -> x0, waiting for transfers between devices: 45.3 us -> none  [the longest x1 22.7 us: body(): lax.psum_scatter(partials[3], 'dp', scatter_dimension=0, tiled=True)]
    add x17 -> x0, other arithmetic: 18 us -> none  [the longest x11 13.4 us: backward_tick(): new_gains.append(gain_sums[role] + jnp.sum(back_norm * normed, axis=0))]
  transfers between devices with their start and end apart: 65 -> 0, of which waited for: 23 -> 0; matrix products, arithmetic and copies ran while one was open for 28% -> 0% of each run, Pallas kernels for 0% -> 0%
where the time goes in v1:
time: 96.6 us; the launch traced here: 96.4 us
  Pallas kernels  87.8 us (91%)
  local copies, waits for them, and re-layouts  7.86 us (8%)
    pallas_call x1, Pallas kernels, body(): pl.pallas_call(functools.partial(kernel, segments, replicas, loss_scale),...  87.8 us
    unnamed x13, local copies, waits for them, and re-layouts  7.86 us

profile of v1, /device:TPU:0, one launch (start us, length us, event | category | flops | bytes accessed | tf_op | source)
XLA Modules:
  0.0 96.4 jit_solution(9988128104622836153)
XLA Ops:
  0.6 0.0 copy-start
  0.6 1.6 %copy-done = bf16[2,512,1024]{2,1,0:T(8,128)(2,1)S(1)} copy-done((bf16[2,512,1024]{2,1,0:T(8,128)(2,1)S(1)}, bf16[2,512,1024]{2,1,0:T(8,128)(2,1)}, u32[]{:S(2)}) %copy-start) | copy-done | bytes 2097176
  2.2 0.0 copy-start.1
  2.2 1.6 %copy-done.1 = bf16[2,1024,512]{2,1,0:T(8,128)(2,1)S(1)} copy-done((bf16[2,1024,512]{2,1,0:T(8,128)(2,1)S(1)}, bf16[2,1024,512]{2,1,0:T(8,128)(2,1)}, u32[]{:S(2)}) %copy-start.1) | copy-done | bytes 2097176
  3.8 0.0 copy-start.2
  3.8 0.9 copy-done.2
  4.8 0.0 copy-start.3
  4.8 0.9 copy-done.3
  5.7 0.0 copy-start.4
  5.7 0.7 copy-done.4
  6.4 87.8 %relay.1 = (f32[256,512]{1,0:T(8,128)S(1)}, f32[512,256]{1,0:T(8,128)S(1)}, f32[1,128]{1,0:T(1,128)S(1)}) custom-call(bf16[4,64,512]{2,1,0:T(8,128)(2,1)S(1)} %copy-done.2, bf16[4,64,512]{2,1,0:T(8,128)(2,1)S(1)} %copy-done.3, bf16[2,512,1024]{2,1,0:T(8,128)(2,1)S(1)} %copy-done, bf16[2,1024,512]{2,1,0:T(8,128)(2,1)S(1)} %copy-done.1, f32[2,512]{1,0:T(2,128)S(1)} %copy-done.4), custom_call_target="tpu_custom_call" | custom-call | flops 1610612736 | bytes 6291456 | tf_op jit(solution)/shard_map/relay/pallas_call | solution.py:340
  94.3 0.8 copy.11
  95.1 0.8 copy.12
  95.9 0.5 copy.13
Async XLA Ops:
  0.6 1.6 %copy-start = (bf16[2,512,1024]{2,1,0:T(8,128)(2,1)S(1)}, bf16[2,512,1024]{2,1,0:T(8,128)(2,1)}, u32[]{:S(2)}) copy-start(bf16[2,512,1024]{2,1,0:T(8,128)(2,1)} %up_hbm.1) | copy-start | bytes 6291460
  2.2 1.6 %copy-start.1 = (bf16[2,1024,512]{2,1,0:T(8,128)(2,1)S(1)}, bf16[2,1024,512]{2,1,0:T(8,128)(2,1)}, u32[]{:S(2)}) copy-start(bf16[2,1024,512]{2,1,0:T(8,128)(2,1)} %down_hbm.1) | copy-start | bytes 6291460
  3.8 0.9 copy-start.2
  4.8 0.9 copy-start.3
  5.7 0.7 copy-start.4

commit v2 on v1

v2 whole, which is shorter than its diff:
```python
import functools
import math

import jax
import jax.numpy as jnp
from jax import lax
from jax.experimental import pallas as pl
from jax.experimental.pallas import tpu as pltpu
from jax.sharding import PartitionSpec as P

GELU_C = 0.7978845608028654
CUBIC = 0.044715
CHUNKS_PER_RELAY = 4
MESH = pl.DeviceIdType.MESH


def dot_tn(left, right):
    return lax.dot_general(left, right, (((0,), (0,)), ((), ())), preferred_element_type=jnp.float32)


def gelu_parts(pre_act):
    tangent = jnp.tanh(GELU_C * (pre_act + CUBIC * pre_act * pre_act * pre_act))
    value = 0.5 * pre_act * (1.0 + tangent)
    slope = 0.5 * (1.0 + tangent) + 0.5 * pre_act * (1.0 - tangent * tangent) * GELU_C * (
        1.0 + 3.0 * CUBIC * pre_act * pre_act
    )
    return value.astype(jnp.bfloat16), slope


def norm_parts(x):
    xc = x - jnp.mean(x, axis=-1, keepdims=True)
    inverse = lax.rsqrt(jnp.mean(xc * xc, axis=-1, keepdims=True) + 1e-05)
    return xc * inverse, inverse


def kernel(
    segments,
    replicas,
    loss_scale,
    rising,
    falling,
    up_hbm,
    down_hbm,
    gain_hbm,
    out_up,
    out_down,
    out_gain,
    up,
    down,
    up_t,
    down_t,
    gain_ref,
    x_all,
    dy_all,
    y_out,
    dx_out,
    xh_st,
    inv_st,
    p_st,
    slope_st,
    da_st,
    n_all,
    p_all,
    slope_all,
    da_all,
    gain_acc,
    acc_up,
    acc_down,
    load_sem,
    feed_sem,
    fs_sem,
    bs_sem,
    xs_sem,
    xr_sem,
    ds_sem,
    dr_sem,
    gs_sem,
    gr_sem,
):
    place = lax.axis_index("segment")
    rep = lax.axis_index("dp")
    pair = place // 2
    core = place % 2
    last = segments // 2 - 1
    slots, chunks, rows, width = x_all.shape
    total = chunks * rows
    half = up.shape[1] // 2
    micro = rising.shape[0]
    local_rows = rising.shape[1] // 2
    mate = place + 1 - 2 * core
    slice_d = width // replicas
    per_chunk = rows // local_rows
    mine = pl.ds(pl.multiple_of(core * half, half), half)

    def feed_copy(which, m):
        flat = which * micro + m
        return pltpu.make_async_copy(
            (rising, falling)[which].at[
                m, pl.ds(pl.multiple_of(core * local_rows, local_rows), local_rows), :
            ],
            x_all.at[0, flat // per_chunk, pl.ds((flat % per_chunk) * local_rows, local_rows), :],
            feed_sem.at[flat],
        )

    load_gain = pltpu.make_async_copy(gain_hbm, gain_ref, load_sem.at[2])
    load_up = pltpu.make_async_copy(up_hbm.at[0], up, load_sem.at[0])
    load_down = pltpu.make_async_copy(down_hbm.at[0], down, load_sem.at[1])

    @pl.when(pair == 0)
    def _():
        for which in (0, 1):
            for m in range(micro):
                feed_copy(which, m).start()

    load_gain.start()
    load_up.start()
    load_down.start()

    peers = [(1, {"segment": mate})]
    for off in range(1, replicas):
        other = lax.rem(rep + off, replicas)
        peers.append((2 * off, {"dp": other}))
        peers.append((2 * off + 1, {"dp": other, "segment": mate}))

    barrier = pltpu.get_barrier_semaphore()

    @pl.when(pair > 0)
    def _():
        pl.semaphore_signal(barrier, inc=1, device_id={"segment": place - 2}, device_id_type=MESH)

    @pl.when(pair < last)
    def _():
        pl.semaphore_signal(barrier, inc=1, device_id={"segment": place + 2}, device_id_type=MESH)

    for _, peer in peers:
        pl.semaphore_signal(barrier, inc=1, device_id=peer, device_id_type=MESH)
    gain_acc[0] = jnp.zeros(gain_acc.shape[1:], gain_acc.dtype)
    pl.semaphore_wait(
        barrier,
        len(peers) + jnp.where(pair > 0, 1, 0) + jnp.where(pair < last, 1, 0),
    )

    def send(src, dst, send_sem, recv_sem, peer):
        return pltpu.make_async_remote_copy(
            src_ref=src,
            dst_ref=dst,
            send_sem=send_sem,
            recv_sem=recv_sem,
            device_id=peer,
            device_id_type=MESH,
        )

    def send_forward(i):
        return send(
            y_out.at[i], x_all.at[0, i], fs_sem.at[i], xr_sem.at[0, i], {"segment": place + 2}
        )

    def send_backward(i):
        return send(
            dx_out.at[i], dy_all.at[0, i], bs_sem.at[i], dr_sem.at[0, i], {"segment": place - 2}
        )

    def share(buf, sems, slot, i):
        if slot == 1:
            peer, origin = {"segment": mate}, 0
        elif slot % 2 == 0:
            peer, origin = {"dp": lax.rem(rep + slot // 2, replicas)}, 0
        else:
            peer, origin = {"segment": mate}, slot - 1
        return send(
            buf.at[origin, i], buf.at[slot, i], sems[0].at[slot, i], sems[1].at[slot, i], peer
        )

    xs = (xs_sem, xr_sem)
    ds = (ds_sem, dr_sem)

    def share_own(buf, sems, i):
        for off in range(1, replicas):
            share(buf, sems, 2 * off, i).start()
        share(buf, sems, 1, i).start()

    def hand_on(buf, sems, i):
        for off in range(1, replicas):
            share(buf, sems, 2 * off, i).wait_recv()
            share(buf, sems, 2 * off + 1, i).start()

    def span(i):
        return pl.ds(pl.multiple_of(i * rows, rows), rows)

    def slot_span(s):
        return pl.ds(pl.multiple_of(s * total, total), total)

    def transpose_weights():
        down_t[...] = down[...].T
        up_t[...] = up[...].T

    @pl.when(pair == 0)
    def _():
        for which in (0, 1):
            for m in range(micro):
                feed_copy(which, m).wait()

    load_gain.wait()
    load_up.wait()
    load_down.wait()
    gain_row = gain_ref[0:1, :]

    @pl.when(2 * pair > last)
    def _():
        transpose_weights()

    def forward(i, carry):
        @pl.when(pair > 0)
        def _():
            send_forward(i).wait_recv()

        x = x_all[0, i].astype(jnp.float32)
        xh, inverse = norm_parts(x)
        n = (xh * gain_row).astype(jnp.bfloat16)
        a = jnp.dot(n, up[...], preferred_element_type=jnp.float32)
        p, slope = gelu_parts(a)
        y = (x + jnp.dot(p, down[...], preferred_element_type=jnp.float32)).astype(jnp.bfloat16)

        @pl.when(pair < last)
        def _():
            y_out[i] = y
            send_forward(i).start()

        @pl.when(pair == last)
        def _():
            dy_all[0, i] = (y.astype(jnp.float32) * loss_scale).astype(jnp.bfloat16)

        share_own(x_all, xs, i)

        @pl.when(i > 0)
        def _():
            hand_on(x_all, xs, i - 1)

        xh_st[i] = xh
        inv_st[i] = jnp.broadcast_to(inverse, (rows, 128))
        n_all[span(i), :] = n
        p_st[span(i), :] = p
        slope_st[i] = slope
        return carry

    lax.fori_loop(0, chunks, forward, 0)
    hand_on(x_all, xs, chunks - 1)

    @pl.when(2 * pair <= last)
    def _():
        transpose_weights()

    def peers_forward():
        for s in range(1, slots, 2):
            for i in range(chunks):
                share(x_all, xs, s, i).wait_recv()

        def one(s, carry):
            xh, _ = norm_parts(x_all[s].reshape(total, width).astype(jnp.float32))
            n = (xh * gain_row).astype(jnp.bfloat16)
            n_all[slot_span(s), :] = n
            a = jnp.dot(n, up[:, mine], preferred_element_type=jnp.float32)
            p, slope = gelu_parts(a)
            p_all[slot_span(s), :] = p
            slope_all[slot_span(s), :] = slope
            return carry

        lax.fori_loop(1, slots, one, 0)
        p_all[slot_span(0), :] = p_st[:, mine]

    @pl.when(pair < last - 1)
    def _():
        peers_forward()

    def backward(i, carry):
        @pl.when(pair < last)
        def _():
            send_backward(i).wait_recv()

        share_own(dy_all, ds, i)
        dy = dy_all[0, i]
        dp = jnp.dot(dy, down_t[...], preferred_element_type=jnp.float32)
        da = (dp * slope_st[i]).astype(jnp.bfloat16)
        dn = jnp.dot(da, up_t[...], preferred_element_type=jnp.float32)
        xh = xh_st[i]
        e = dn * gain_row
        m1 = jnp.mean(e, axis=-1, keepdims=True)
        m2 = jnp.mean(e * xh, axis=-1, keepdims=True)
        inverse = inv_st[i][:, 0:1]
        dx = (dy.astype(jnp.float32) + inverse * (e - m1 - xh * m2)).astype(jnp.bfloat16)

        @pl.when(pair > 0)
        def _():
            dx_out[i] = dx
            send_backward(i).start()

        @pl.when(i > 0)
        def _():
            hand_on(dy_all, ds, i - 1)

        da_st[span(i), :] = da
        gain_acc[0] += jnp.sum((dn * xh).reshape(rows // 8, 8, width), axis=0)
        return carry

    lax.fori_loop(0, chunks, backward, 0)
    hand_on(dy_all, ds, chunks - 1)

    def send_gain(slot, peer):
        return send(gain_acc.at[0], gain_acc.at[slot], gs_sem.at[slot], gr_sem.at[slot], peer)

    for slot, peer in peers:
        send_gain(slot, peer).start()

    @pl.when(pair >= last - 1)
    def _():
        peers_forward()

    da_all[slot_span(0), :] = da_st[:, mine]
    for s in range(2, slots, 2):
        peer_da(s, slot_span, dy_all, down_t, mine, slope_all, da_all)
    for s in range(1, slots, 2):
        for i in range(chunks):
            share(dy_all, ds, s, i).wait_recv()
        peer_da(s, slot_span, dy_all, down_t, mine, slope_all, da_all)

    if slice_d % 128 == 0:
        cols = pl.ds(pl.multiple_of(rep * slice_d, slice_d), slice_d)
        out_up[...] = dot_tn(n_all[:, cols], da_all[...])
        dy_cols = dy_all[:, :, :, cols].reshape(slots * total, slice_d)
        out_down[...] = dot_tn(p_all[...], dy_cols)
    else:
        whole_up = dot_tn(n_all[...], da_all[...])
        whole_down = dot_tn(p_all[...], dy_all[...].reshape(slots * total, width))
        for j in range(replicas):
            acc_up[j] = whole_up[j * slice_d : (j + 1) * slice_d, :]
            acc_down[j] = whole_down[:, j * slice_d : (j + 1) * slice_d]
        out_up[...] = acc_up[rep]
        out_down[...] = acc_down[rep]

    gains = gain_acc[0]
    for slot, peer in peers:
        send_gain(slot, peer).wait()
        gains = gains + gain_acc[slot]
    gains = jnp.sum(gains, axis=0, keepdims=True)
    wide = out_gain.shape[1]
    for c in (0, 1):
        for j in range(replicas):
            start = c * (width // 2) + j * wide

            @pl.when((core == c) & (rep == j))
            def _():
                out_gain[...] = gains[:, start : start + wide]

    def drain(i, carry):
        for slot in range(1, slots):
            share(x_all, xs, slot, i).wait_send()
            share(dy_all, ds, slot, i).wait_send()

        @pl.when(pair < last)
        def _():
            send_forward(i).wait_send()

        @pl.when(pair > 0)
        def _():
            send_backward(i).wait_send()

        return carry

    lax.fori_loop(0, chunks, drain, 0)


def peer_da(s, slot_span, dy_all, down_t, mine, slope_all, da_all):
    slots, chunks, rows, width = dy_all.shape
    dy = dy_all[s].reshape(chunks * rows, width)
    dp = jnp.dot(dy, down_t[:, mine], preferred_element_type=jnp.float32)
    da_all[slot_span(s), :] = (dp * slope_all[slot_span(s), :]).astype(jnp.bfloat16)


def body(feed_rising, feed_falling, up_weight, down_weight, norm_gain):
    segments = lax.axis_size("segment")
    replicas = lax.axis_size("dp")
    micro, rep_rows, width = feed_rising.shape
    local_rows = rep_rows // 2
    hidden = up_weight.shape[2]
    half = hidden // 2
    loss_scale = 1.0 / math.sqrt(2.0 * micro * rep_rows * replicas)
    chunks = 2 * CHUNKS_PER_RELAY
    rows = 2 * micro * local_rows // chunks
    total = chunks * rows
    slots = 2 * replicas
    slice_d = width // replicas
    bf16, f32 = jnp.bfloat16, jnp.float32
    vmem = pl.BlockSpec(memory_space=pltpu.VMEM)
    hbm = pl.BlockSpec(memory_space=pltpu.HBM)
    spare = (8, 128) if slice_d % 128 == 0 else None
    dma = pltpu.SemaphoreType.DMA
    return pl.pallas_call(
        functools.partial(kernel, segments, replicas, loss_scale),
        out_shape=(
            jax.ShapeDtypeStruct((slice_d, half), f32),
            jax.ShapeDtypeStruct((half, slice_d), f32),
            jax.ShapeDtypeStruct((1, width // 2 // replicas), f32),
        ),
        in_specs=[hbm, hbm, hbm, hbm, hbm],
        out_specs=(vmem, vmem, vmem),
        scratch_shapes=[
            pltpu.VMEM((width, hidden), bf16),
            pltpu.VMEM((hidden, width), bf16),
            pltpu.VMEM((hidden, width), bf16),
            pltpu.VMEM((width, hidden), bf16),
            pltpu.VMEM((norm_gain.shape[0], width), f32),
            pltpu.VMEM((slots, chunks, rows, width), bf16),
            pltpu.VMEM((slots, chunks, rows, width), bf16),
            pltpu.VMEM((chunks, rows, width), bf16),
            pltpu.VMEM((chunks, rows, width), bf16),
            pltpu.VMEM((chunks, rows, width), f32),
            pltpu.VMEM((chunks, rows, 128), f32),
            pltpu.VMEM((total, hidden), bf16),
            pltpu.VMEM((chunks, rows, hidden), f32),
            pltpu.VMEM((total, hidden), bf16),
            pltpu.VMEM((slots * total, width), bf16),
            pltpu.VMEM((slots * total, half), bf16),
            pltpu.VMEM((slots * total, half), f32),
            pltpu.VMEM((slots * total, half), bf16),
            pltpu.VMEM((slots, 8, width), f32),
            pltpu.VMEM(spare or (replicas, slice_d, half), f32),
            pltpu.VMEM(spare or (replicas, half, slice_d), f32),
            dma((3,)),
            dma((2 * micro,)),
            dma((chunks,)),
            dma((chunks,)),
            dma((slots, chunks)),
            dma((slots, chunks)),
            dma((slots, chunks)),
            dma((slots, chunks)),
            dma((slots,)),
            dma((slots,)),
        ],
        compiler_params=pltpu.CompilerParams(
            collective_id=0, has_side_effects=True, vmem_limit_bytes=56 * 1024 * 1024
        ),
        cost_estimate=pl.CostEstimate(
            flops=16 * total * width * hidden,
            bytes_accessed=6 * 1024 * 1024,
            transcendentals=3 * total * hidden,
        ),
        name="relay",
    )(feed_rising, feed_falling, up_weight, down_weight, norm_gain)


def solution(mesh):
    return jax.shard_map(
        body,
        mesh=mesh,
        in_specs=(
            P(None, "dp", None),
            P(None, "dp", None),
            P("segment", None, None),
            P("segment", None, None),
            P("segment", None),
        ),
        out_specs=(P("dp", "segment"), P("segment", "dp"), P("segment", "dp")),
        check_vma=False,
    )
```

time: 96.6 us -> 94.7 us (0.980)
  local copies, waits for them, and re-layouts: 7.86 us -> 4.25 us
  Pallas kernels: 87.8 us -> 89.6 us
    unnamed x13 -> x5, local copies, waits for them, and re-layouts: 7.86 us -> 4.25 us
    pallas_call x1, Pallas kernels: 87.8 us -> 89.6 us  [body(): pl.pallas_call(functools.partial(kernel, segments, replicas, loss_scale),...]
where the time goes in v2:
time: 94.7 us; the launch traced here: 94.5 us
  Pallas kernels  89.6 us (95%)
  local copies, waits for them, and re-layouts  4.25 us (4%)
    pallas_call x1, Pallas kernels, body(): pl.pallas_call(functools.partial(kernel, segments, replicas, loss_scale),...  89.6 us
    unnamed x5, local copies, waits for them, and re-layouts  4.25 us

profile of v2, /device:TPU:0, one launch (start us, length us, event | category | flops | bytes accessed | tf_op | source)
XLA Modules:
  0.0 94.5 jit_solution(1850489293949232378)
XLA Ops:
  0.6 89.6 %relay.1 = (f32[256,512]{1,0:T(8,128)}, f32[512,256]{1,0:T(8,128)}, f32[1,128]{1,0:T(1,128)}) custom-call(bf16[4,64,512]{2,1,0:T(8,128)(2,1)} %rising.1, bf16[4,64,512]{2,1,0:T(8,128)(2,1)} %falling.1, bf16[2,512,1024]{2,1,0:T(8,128)(2,1)} %up_hbm.1, bf16[2,1024,512]{2,1,0:T(8,128)(2,1)} %down_hbm.1, f32[2,512]{1,0:T(2,128)} %gain_hbm.1), custom_call_target="tpu_custom_call" | custom-call | flops 2147483648 | bytes 6291456 | tf_op jit(solution)/shard_map/relay/pallas_call | solution.py:397
  90.2 0.0 copy-start
  90.2 1.9 %copy.11 = f32[256,512]{1,0:T(8,128)} copy(f32[256,512]{1,0:T(8,128)} %get-tuple-element.6) | data formatting | bytes 1048576
  92.1 1.9 %copy.12 = f32[512,256]{1,0:T(8,128)} copy(f32[512,256]{1,0:T(8,128)} %get-tuple-element.7) | data formatting | bytes 1048576
  94.0 0.0 copy-done
  94.0 0.5 copy.13
Async XLA Ops:
  90.2 3.7 %copy-start = (f32[1,128]{1,0:T(1,128)S(1)}, f32[1,128]{1,0:T(1,128)}, u32[]{:S(2)}) copy-start(f32[1,128]{1,0:T(1,128)} %get-tuple-element.8) | copy-start | bytes 1540

commit v3 on v2

--- a/solution.py
+++ b/solution.py
@@ -10,21 +10,25 @@
 
 GELU_C = 0.7978845608028654
 CUBIC = 0.044715
-CHUNKS_PER_RELAY = 4
+CHUNKS_PER_RELAY = 2
+TILE = 256
 MESH = pl.DeviceIdType.MESH
 
 
 def dot_tn(left, right):
     return lax.dot_general(left, right, (((0,), (0,)), ((), ())), preferred_element_type=jnp.float32)
+
+
+def gelu_slope(pre_act, tangent):
+    return 0.5 * (1.0 + tangent) + 0.5 * pre_act * (1.0 - tangent * tangent) * GELU_C * (
+        1.0 + 3.0 * CUBIC * pre_act * pre_act
+    )
 
 
 def gelu_parts(pre_act):
     tangent = jnp.tanh(GELU_C * (pre_act + CUBIC * pre_act * pre_act * pre_act))
     value = 0.5 * pre_act * (1.0 + tangent)
-    slope = 0.5 * (1.0 + tangent) + 0.5 * pre_act * (1.0 - tangent * tangent) * GELU_C * (
-        1.0 + 3.0 * CUBIC * pre_act * pre_act
-    )
-    return value.astype(jnp.bfloat16), slope
+    return value.astype(jnp.bfloat16), gelu_slope(pre_act, tangent)
 
 
 def norm_parts(x):
@@ -58,6 +62,8 @@
     inv_st,
     p_st,
     slope_st,
+    a_st,
+    t_st,
     da_st,
     n_all,
     p_all,
@@ -217,9 +223,16 @@
         x = x_all[0, i].astype(jnp.float32)
         xh, inverse = norm_parts(x)
         n = (xh * gain_row).astype(jnp.bfloat16)
-        a = jnp.dot(n, up[...], preferred_element_type=jnp.float32)
-        p, slope = gelu_parts(a)
-        y = (x + jnp.dot(p, down[...], preferred_element_type=jnp.float32)).astype(jnp.bfloat16)
+        y = x
+        for j in range(0, 2 * half, TILE):
+            a = jnp.dot(n, up[:, j : j + TILE], preferred_element_type=jnp.float32)
+            t = jnp.tanh(GELU_C * (a + CUBIC * a * a * a))
+            p = (0.5 * a * (1.0 + t)).astype(jnp.bfloat16)
+            a_st[:, j : j + TILE] = a
+            t_st[:, j : j + TILE] = t
+            p_st[span(i), j : j + TILE] = p
+            y = y + jnp.dot(p, down[j : j + TILE, :], preferred_element_type=jnp.float32)
+        y = y.astype(jnp.bfloat16)
 
         @pl.when(pair < last)
         def _():
@@ -239,8 +252,7 @@
         xh_st[i] = xh
         inv_st[i] = jnp.broadcast_to(inverse, (rows, 128))
         n_all[span(i), :] = n
-        p_st[span(i), :] = p
-        slope_st[i] = slope
+        slope_st[i] = gelu_slope(a_st[...], t_st[...])
         return carry
 
     lax.fori_loop(0, chunks, forward, 0)
@@ -277,11 +289,13 @@
         def _():
             send_backward(i).wait_recv()
 
-        share_own(dy_all, ds, i)
         dy = dy_all[0, i]
-        dp = jnp.dot(dy, down_t[...], preferred_element_type=jnp.float32)
-        da = (dp * slope_st[i]).astype(jnp.bfloat16)
-        dn = jnp.dot(da, up_t[...], preferred_element_type=jnp.float32)
+        dn = jnp.zeros((rows, width), jnp.float32)
+        for j in range(0, 2 * half, TILE):
+            dp = jnp.dot(dy, down_t[:, j : j + TILE], preferred_element_type=jnp.float32)
+            da = (dp * slope_st[i, :, j : j + TILE]).astype(jnp.bfloat16)
+            da_st[span(i), j : j + TILE] = da
+            dn = dn + jnp.dot(da, up_t[j : j + TILE, :], preferred_element_type=jnp.float32)
         xh = xh_st[i]
         e = dn * gain_row
         m1 = jnp.mean(e, axis=-1, keepdims=True)
@@ -294,11 +308,12 @@
             dx_out[i] = dx
             send_backward(i).start()
 
+        share_own(dy_all, ds, i)
+
         @pl.when(i > 0)
         def _():
             hand_on(dy_all, ds, i - 1)
 
-        da_st[span(i), :] = da
         gain_acc[0] += jnp.sum((dn * xh).reshape(rows // 8, 8, width), axis=0)
         return carry
 
@@ -417,6 +432,8 @@
             pltpu.VMEM((chunks, rows, 128), f32),
             pltpu.VMEM((total, hidden), bf16),
             pltpu.VMEM((chunks, rows, hidden), f32),
+            pltpu.VMEM((rows, hidden), f32),
+            pltpu.VMEM((rows, hidden), f32),
             pltpu.VMEM((total, hidden), bf16),
             pltpu.VMEM((slots * total, width), bf16),
             pltpu.VMEM((slots * total, half), bf16),
@@ -437,7 +454,7 @@
             dma((slots,)),
         ],
         compiler_params=pltpu.CompilerParams(
-            collective_id=0, has_side_effects=True, vmem_limit_bytes=56 * 1024 * 1024
+            collective_id=0, has_side_effects=True, vmem_limit_bytes=(24 + 2 * slots) * 1024 * 1024
         ),
         cost_estimate=pl.CostEstimate(
             flops=16 * total * width * hidden,

time: 94.7 us -> 96.9 us (1.023)
  local copies, waits for them, and re-layouts: 4.25 us -> 7.86 us
  Pallas kernels: 89.6 us -> 87.9 us
    unnamed x5 -> x13, local copies, waits for them, and re-layouts: 4.25 us -> 7.86 us
    pallas_call x1, Pallas kernels: 89.6 us -> 87.9 us  [body(): pl.pallas_call(functools.partial(kernel, segments, replicas, loss_scale),...]
where the time goes in v3:
time: 96.9 us; the launch traced here: 96.5 us
  Pallas kernels  87.9 us (91%)
  local copies, waits for them, and re-layouts  7.86 us (8%)
    pallas_call x1, Pallas kernels, body(): pl.pallas_call(functools.partial(kernel, segments, replicas, loss_scale),...  87.9 us
    unnamed x13, local copies, waits for them, and re-layouts  7.86 us

profile of v3, /device:TPU:0, one launch (start us, length us, event | category | flops | bytes accessed | tf_op | source)
XLA Modules:
  0.0 96.5 jit_solution(5128679026201910792)
XLA Ops:
  0.6 0.0 copy-start
  0.6 1.6 %copy-done = bf16[2,512,1024]{2,1,0:T(8,128)(2,1)S(1)} copy-done((bf16[2,512,1024]{2,1,0:T(8,128)(2,1)S(1)}, bf16[2,512,1024]{2,1,0:T(8,128)(2,1)}, u32[]{:S(2)}) %copy-start) | copy-done | bytes 2097176
  2.2 0.0 copy-start.1
  2.2 1.6 %copy-done.1 = bf16[2,1024,512]{2,1,0:T(8,128)(2,1)S(1)} copy-done((bf16[2,1024,512]{2,1,0:T(8,128)(2,1)S(1)}, bf16[2,1024,512]{2,1,0:T(8,128)(2,1)}, u32[]{:S(2)}) %copy-start.1) | copy-done | bytes 2097176
  3.8 0.0 copy-start.2
  3.8 0.9 copy-done.2
  4.8 0.0 copy-start.3
  4.8 0.9 copy-done.3
  5.7 0.0 copy-start.4
  5.7 0.7 copy-done.4
  6.4 87.9 %relay.1 = (f32[256,512]{1,0:T(8,128)S(1)}, f32[512,256]{1,0:T(8,128)S(1)}, f32[1,128]{1,0:T(1,128)S(1)}) custom-call(bf16[4,64,512]{2,1,0:T(8,128)(2,1)S(1)} %copy-done.2, bf16[4,64,512]{2,1,0:T(8,128)(2,1)S(1)} %copy-done.3, bf16[2,512,1024]{2,1,0:T(8,128)(2,1)S(1)} %copy-done, bf16[2,1024,512]{2,1,0:T(8,128)(2,1)S(1)} %copy-done.1, f32[2,512]{1,0:T(2,128)S(1)} %copy-done.4), custom_call_target="tpu_custom_call" | custom-call | flops 2147483648 | bytes 6291456 | tf_op jit(solution)/shard_map/relay/pallas_call | solution.py:412
  94.4 0.8 copy.11
  95.2 0.8 copy.12
  95.9 0.5 copy.13
Async XLA Ops:
  0.6 1.6 %copy-start = (bf16[2,512,1024]{2,1,0:T(8,128)(2,1)S(1)}, bf16[2,512,1024]{2,1,0:T(8,128)(2,1)}, u32[]{:S(2)}) copy-start(bf16[2,512,1024]{2,1,0:T(8,128)(2,1)} %up_hbm.1) | copy-start | bytes 6291460
  2.2 1.6 %copy-start.1 = (bf16[2,1024,512]{2,1,0:T(8,128)(2,1)S(1)}, bf16[2,1024,512]{2,1,0:T(8,128)(2,1)}, u32[]{:S(2)}) copy-start(bf16[2,1024,512]{2,1,0:T(8,128)(2,1)} %down_hbm.1) | copy-start | bytes 6291460
  3.8 0.9 copy-start.2
  4.8 0.9 copy-start.3
  5.7 0.7 copy-start.4

commit v4 on v3

--- a/solution.py
+++ b/solution.py
@@ -289,6 +289,10 @@
         def _():
             send_backward(i).wait_recv()
 
+        @pl.when(pair == 0)
+        def _():
+            share_own(dy_all, ds, i)
+
         dy = dy_all[0, i]
         dn = jnp.zeros((rows, width), jnp.float32)
         for j in range(0, 2 * half, TILE):
@@ -307,8 +311,7 @@
         def _():
             dx_out[i] = dx
             send_backward(i).start()
-
-        share_own(dy_all, ds, i)
+            share_own(dy_all, ds, i)
 
         @pl.when(i > 0)
         def _():
@@ -382,6 +385,15 @@
         return carry
 
     lax.fori_loop(0, chunks, drain, 0)
+
+
+def hand_over(*refs):
+    sem = refs[6]
+    copies = [pltpu.make_async_copy(refs[k], refs[3 + k], sem.at[k]) for k in range(3)]
+    for copy in copies:
+        copy.start()
+    for copy in copies:
+        copy.wait()
 
 
 def peer_da(s, slot_span, dy_all, down_t, mine, slope_all, da_all):
@@ -409,7 +421,7 @@
     hbm = pl.BlockSpec(memory_space=pltpu.HBM)
     spare = (8, 128) if slice_d % 128 == 0 else None
     dma = pltpu.SemaphoreType.DMA
-    return pl.pallas_call(
+    grads = pl.pallas_call(
         functools.partial(kernel, segments, replicas, loss_scale),
         out_shape=(
             jax.ShapeDtypeStruct((slice_d, half), f32),
@@ -454,7 +466,7 @@
             dma((slots,)),
         ],
         compiler_params=pltpu.CompilerParams(
-            collective_id=0, has_side_effects=True, vmem_limit_bytes=(24 + 2 * slots) * 1024 * 1024
+            collective_id=0, has_side_effects=True, vmem_limit_bytes=60 * 1024 * 1024
         ),
         cost_estimate=pl.CostEstimate(
             flops=16 * total * width * hidden,
@@ -463,6 +475,15 @@
         ),
         name="relay",
     )(feed_rising, feed_falling, up_weight, down_weight, norm_gain)
+    return pl.pallas_call(
+        hand_over,
+        out_shape=tuple(jax.ShapeDtypeStruct(g.shape, g.dtype) for g in grads),
+        in_specs=[hbm] * 3,
+        out_specs=(hbm,) * 3,
+        scratch_shapes=[dma((3,))],
+        compiler_params=pltpu.CompilerParams(vmem_limit_bytes=60 * 1024 * 1024),
+        name="hand_over",
+    )(*grads)
 
 
 def solution(mesh):

time: 96.9 us -> 123 us (1.27)
  Pallas kernels: 87.9 us -> 122 us
  local copies, waits for them, and re-layouts: 7.86 us -> 0 us
    pallas_call x0 -> x1, Pallas kernels: none -> 32.9 us  [body(): pl.pallas_call(hand_over, out_shape=tuple((jax.ShapeDtypeStruct(g.shape,...]
    unnamed x13 -> x0, local copies, waits for them, and re-layouts: 7.86 us -> none
    pallas_call x1, Pallas kernels: 87.9 us -> 89.5 us  [body(): pl.pallas_call(functools.partial(kernel, segments, replicas, loss_scale),...]
where the time goes in v4:
time: 123 us
  Pallas kernels  122 us (99%)
    pallas_call x1, Pallas kernels, body(): pl.pallas_call(functools.partial(kernel, segments, replicas, loss_scale),...  89.5 us
    pallas_call x1, Pallas kernels, body(): pl.pallas_call(hand_over, out_shape=tuple((jax.ShapeDtypeStruct(g.shape,...  32.9 us

profile of v4, /device:TPU:0, one launch (start us, length us, event | category | flops | bytes accessed | tf_op | source)
XLA Modules:
  0.0 123.0 jit_solution(12199895153944245166)
XLA Ops:
  0.6 89.5 %relay.1 = (f32[256,512]{1,0:T(8,128)}, f32[512,256]{1,0:T(8,128)}, f32[1,128]{1,0:T(1,128)}) custom-call(bf16[4,64,512]{2,1,0:T(8,128)(2,1)} %rising.1, bf16[4,64,512]{2,1,0:T(8,128)(2,1)} %falling.1, bf16[2,512,1024]{2,1,0:T(8,128)(2,1)} %up_hbm.1, bf16[2,1024,512]{2,1,0:T(8,128)(2,1)} %down_hbm.1, f32[2,512]{1,0:T(2,128)} %gain_hbm.1), custom_call_target="tpu_custom_call" | custom-call | flops 2147483648 | bytes 6291456 | tf_op jit(solution)/shard_map/relay/pallas_call | solution.py:424
  90.1 32.9 %hand_over.1 = (f32[256,512]{1,0:T(8,128)}, f32[512,256]{1,0:T(8,128)}, f32[1,128]{1,0:T(1,128)}) custom-call(f32[256,512]{1,0:T(8,128)} %get-tuple-element.6.refs_0_, f32[512,256]{1,0:T(8,128)} %get-tuple-element.7.refs_1_, f32[1,128]{1,0:T(1,128)} %get-tuple-element.8.refs_2_), custom_call_target="tpu_custom_call" | custom-call | tf_op jit(solution)/shard_map/hand_over/pallas_call | solution.py:478

commit v5 on v4

--- a/solution.py
+++ b/solution.py
@@ -10,7 +10,8 @@
 
 GELU_C = 0.7978845608028654
 CUBIC = 0.044715
-CHUNKS_PER_RELAY = 2
+CHUNKS_PER_RELAY = 4
+LAG = 3
 TILE = 256
 MESH = pl.DeviceIdType.MESH
 
@@ -245,10 +246,6 @@
 
         share_own(x_all, xs, i)
 
-        @pl.when(i > 0)
-        def _():
-            hand_on(x_all, xs, i - 1)
-
         xh_st[i] = xh
         inv_st[i] = jnp.broadcast_to(inverse, (rows, 128))
         n_all[span(i), :] = n
@@ -256,7 +253,12 @@
         return carry
 
     lax.fori_loop(0, chunks, forward, 0)
-    hand_on(x_all, xs, chunks - 1)
+
+    def hand_on_rows(i, carry):
+        hand_on(x_all, xs, i)
+        return carry
+
+    lax.fori_loop(0, chunks, hand_on_rows, 0)
 
     @pl.when(2 * pair <= last)
     def _():
@@ -313,15 +315,16 @@
             send_backward(i).start()
             share_own(dy_all, ds, i)
 
-        @pl.when(i > 0)
-        def _():
-            hand_on(dy_all, ds, i - 1)
+        @pl.when(i >= LAG)
+        def _():
+            hand_on(dy_all, ds, i - LAG)
 
         gain_acc[0] += jnp.sum((dn * xh).reshape(rows // 8, 8, width), axis=0)
         return carry
 
     lax.fori_loop(0, chunks, backward, 0)
-    hand_on(dy_all, ds, chunks - 1)
+    for i in range(chunks - LAG, chunks):
+        hand_on(dy_all, ds, i)
 
     def send_gain(slot, peer):
         return send(gain_acc.at[0], gain_acc.at[slot], gs_sem.at[slot], gr_sem.at[slot], peer)
@@ -388,12 +391,8 @@
 
 
 def hand_over(*refs):
-    sem = refs[6]
-    copies = [pltpu.make_async_copy(refs[k], refs[3 + k], sem.at[k]) for k in range(3)]
-    for copy in copies:
-        copy.start()
-    for copy in copies:
-        copy.wait()
+    for k in range(3):
+        refs[3 + k][...] = refs[k][...]
 
 
 def peer_da(s, slot_span, dy_all, down_t, mine, slope_all, da_all):
@@ -478,10 +477,8 @@
     return pl.pallas_call(
         hand_over,
         out_shape=tuple(jax.ShapeDtypeStruct(g.shape, g.dtype) for g in grads),
-        in_specs=[hbm] * 3,
-        out_specs=(hbm,) * 3,
-        scratch_shapes=[dma((3,))],
-        compiler_params=pltpu.CompilerParams(vmem_limit_bytes=60 * 1024 * 1024),
+        in_specs=[vmem] * 3,
+        out_specs=(vmem,) * 3,
         name="hand_over",
     )(*grads)
 

time: 123 us -> 86.1 us (0.70)
  Pallas kernels: 122 us -> 85.3 us
    pallas_call x1, Pallas kernels: 32.9 us -> 2.2 us  [body(): pl.pallas_call(hand_over, out_shape=tuple((jax.ShapeDtypeStruct(g.shape,...]
    pallas_call x1, Pallas kernels: 89.5 us -> 83.1 us  [body(): pl.pallas_call(functools.partial(kernel, segments, replicas, loss_scale),...]
where the time goes in v5:
time: 86.1 us; the launch traced here: 86 us
  Pallas kernels  85.3 us (99%)
    pallas_call x1, Pallas kernels, body(): pl.pallas_call(functools.partial(kernel, segments, replicas, loss_scale),...  83.1 us
    pallas_call x1, Pallas kernels, body(): pl.pallas_call(hand_over, out_shape=tuple((jax.ShapeDtypeStruct(g.shape,...  2.2 us

profile of v5, /device:TPU:0, one launch (start us, length us, event | category | flops | bytes accessed | tf_op | source)
XLA Modules:
  0.0 86.0 jit_solution(2931421380346789864)
XLA Ops:
  0.6 83.1 %relay.1 = (f32[256,512]{1,0:T(8,128)}, f32[512,256]{1,0:T(8,128)}, f32[1,128]{1,0:T(1,128)}) custom-call(bf16[4,64,512]{2,1,0:T(8,128)(2,1)} %rising.1, bf16[4,64,512]{2,1,0:T(8,128)(2,1)} %falling.1, bf16[2,512,1024]{2,1,0:T(8,128)(2,1)} %up_hbm.1, bf16[2,1024,512]{2,1,0:T(8,128)(2,1)} %down_hbm.1, f32[2,512]{1,0:T(2,128)} %gain_hbm.1), custom_call_target="tpu_custom_call" | custom-call | flops 2147483648 | bytes 6291456 | tf_op jit(solution)/shard_map/relay/pallas_call | solution.py:423
  83.8 2.2 %hand_over.1 = (f32[256,512]{1,0:T(8,128)}, f32[512,256]{1,0:T(8,128)}, f32[1,128]{1,0:T(1,128)}) custom-call(f32[256,512]{1,0:T(8,128)} %get-tuple-element.6.refs_0_, f32[512,256]{1,0:T(8,128)} %get-tuple-element.7.refs_1_, f32[1,128]{1,0:T(1,128)} %get-tuple-element.8.refs_2_), custom_call_target="tpu_custom_call" | custom-call | tf_op jit(solution)/shard_map/hand_over/pallas_call | solution.py:477

commit v6 on v5

--- a/solution.py
+++ b/solution.py
@@ -244,8 +244,6 @@
         def _():
             dy_all[0, i] = (y.astype(jnp.float32) * loss_scale).astype(jnp.bfloat16)
 
-        share_own(x_all, xs, i)
-
         xh_st[i] = xh
         inv_st[i] = jnp.broadcast_to(inverse, (rows, 128))
         n_all[span(i), :] = n
@@ -254,17 +252,24 @@
 
     lax.fori_loop(0, chunks, forward, 0)
 
-    def hand_on_rows(i, carry):
-        hand_on(x_all, xs, i)
-        return carry
-
-    lax.fori_loop(0, chunks, hand_on_rows, 0)
-
     @pl.when(2 * pair <= last)
     def _():
         transpose_weights()
 
+    def share_rows(buf, sems):
+        def share_chunk(i, carry):
+            share_own(buf, sems, i)
+            return carry
+
+        def hand_on_chunk(i, carry):
+            hand_on(buf, sems, i)
+            return carry
+
+        lax.fori_loop(0, chunks, share_chunk, 0)
+        lax.fori_loop(0, chunks, hand_on_chunk, 0)
+
     def peers_forward():
+        share_rows(x_all, xs)
         for s in range(1, slots, 2):
             for i in range(chunks):
                 share(x_all, xs, s, i).wait_recv()
@@ -313,9 +318,8 @@
         def _():
             dx_out[i] = dx
             send_backward(i).start()
-            share_own(dy_all, ds, i)
-
-        @pl.when(i >= LAG)
+
+        @pl.when((pair == 0) & (i >= LAG))
         def _():
             hand_on(dy_all, ds, i - LAG)
 
@@ -323,8 +327,14 @@
         return carry
 
     lax.fori_loop(0, chunks, backward, 0)
-    for i in range(chunks - LAG, chunks):
-        hand_on(dy_all, ds, i)
+    @pl.when(pair == 0)
+    def _():
+        for i in range(chunks - LAG, chunks):
+            hand_on(dy_all, ds, i)
+
+    @pl.when(pair > 0)
+    def _():
+        share_rows(dy_all, ds)
 
     def send_gain(slot, peer):
         return send(gain_acc.at[0], gain_acc.at[slot], gs_sem.at[slot], gr_sem.at[slot], peer)

time: 86.1 us -> 82.4 us (0.957)
  Pallas kernels: 85.3 us -> 81.6 us
    pallas_call x1, Pallas kernels: 83.1 us -> 79.4 us  [body(): pl.pallas_call(functools.partial(kernel, segments, replicas, loss_scale),...]
where the time goes in v6:
time: 82.4 us; the launch traced here: 82.3 us
  Pallas kernels  81.6 us (99%)
    pallas_call x1, Pallas kernels, body(): pl.pallas_call(functools.partial(kernel, segments, replicas, loss_scale),...  79.4 us
    pallas_call x1, Pallas kernels, body(): pl.pallas_call(hand_over, out_shape=tuple((jax.ShapeDtypeStruct(g.shape,...  2.2 us

profile of v6, /device:TPU:0, one launch (start us, length us, event | category | flops | bytes accessed | tf_op | source)
XLA Modules:
  0.0 82.3 jit_solution(6861811887747781859)
XLA Ops:
  0.6 79.4 %relay.1 = (f32[256,512]{1,0:T(8,128)}, f32[512,256]{1,0:T(8,128)}, f32[1,128]{1,0:T(1,128)}) custom-call(bf16[4,64,512]{2,1,0:T(8,128)(2,1)} %rising.1, bf16[4,64,512]{2,1,0:T(8,128)(2,1)} %falling.1, bf16[2,512,1024]{2,1,0:T(8,128)(2,1)} %up_hbm.1, bf16[2,1024,512]{2,1,0:T(8,128)(2,1)} %down_hbm.1, f32[2,512]{1,0:T(2,128)} %gain_hbm.1), custom_call_target="tpu_custom_call" | custom-call | flops 2147483648 | bytes 6291456 | tf_op jit(solution)/shard_map/relay/pallas_call | solution.py:433
  80.1 2.2 %hand_over.1 = (f32[256,512]{1,0:T(8,128)}, f32[512,256]{1,0:T(8,128)}, f32[1,128]{1,0:T(1,128)}) custom-call(f32[256,512]{1,0:T(8,128)} %get-tuple-element.6.refs_0_, f32[512,256]{1,0:T(8,128)} %get-tuple-element.7.refs_1_, f32[1,128]{1,0:T(1,128)} %get-tuple-element.8.refs_2_), custom_call_target="tpu_custom_call" | custom-call | tf_op jit(solution)/shard_map/hand_over/pallas_call | solution.py:487

commit v7 on v6

--- a/solution.py
+++ b/solution.py
@@ -77,6 +77,7 @@
     feed_sem,
     fs_sem,
     bs_sem,
+    ac_sem,
     xs_sem,
     xr_sem,
     ds_sem,
@@ -139,12 +140,30 @@
     def _():
         pl.semaphore_signal(barrier, inc=1, device_id={"segment": place + 2}, device_id_type=MESH)
 
+    for off in range(1, replicas):
+        other = lax.rem(rep + off, replicas)
+
+        @pl.when(pair == 0)
+        def _():
+            pl.semaphore_signal(
+                barrier, inc=1, device_id={"dp": other, "segment": place + 2}, device_id_type=MESH
+            )
+
+        @pl.when(pair == 1)
+        def _():
+            pl.semaphore_signal(
+                barrier, inc=1, device_id={"dp": other, "segment": place - 2}, device_id_type=MESH
+            )
+
     for _, peer in peers:
         pl.semaphore_signal(barrier, inc=1, device_id=peer, device_id_type=MESH)
     gain_acc[0] = jnp.zeros(gain_acc.shape[1:], gain_acc.dtype)
     pl.semaphore_wait(
         barrier,
-        len(peers) + jnp.where(pair > 0, 1, 0) + jnp.where(pair < last, 1, 0),
+        len(peers)
+        + jnp.where(pair > 0, 1, 0)
+        + jnp.where(pair < last, 1, 0)
+        + jnp.where(pair <= 1, replicas - 1, 0),
     )
 
     def send(src, dst, send_sem, recv_sem, peer):
@@ -165,6 +184,15 @@
     def send_backward(i):
         return send(
             dx_out.at[i], dy_all.at[0, i], bs_sem.at[i], dr_sem.at[0, i], {"segment": place - 2}
+        )
+
+    def send_across(off, i):
+        return send(
+            dx_out.at[i],
+            dy_all.at[2 * off, i],
+            ac_sem.at[off, i],
+            dr_sem.at[2 * off, i],
+            {"dp": lax.rem(rep + off, replicas), "segment": place - 2},
         )
 
     def share(buf, sems, slot, i):
@@ -298,7 +326,7 @@
 
         @pl.when(pair == 0)
         def _():
-            share_own(dy_all, ds, i)
+            share(dy_all, ds, 1, i).start()
 
         dy = dy_all[0, i]
         dn = jnp.zeros((rows, width), jnp.float32)
@@ -319,6 +347,11 @@
             dx_out[i] = dx
             send_backward(i).start()
 
+        @pl.when(pair == 1)
+        def _():
+            for off in range(1, replicas):
+                send_across(off, i).start()
+
         @pl.when((pair == 0) & (i >= LAG))
         def _():
             hand_on(dy_all, ds, i - LAG)
@@ -385,7 +418,18 @@
     def drain(i, carry):
         for slot in range(1, slots):
             share(x_all, xs, slot, i).wait_send()
-            share(dy_all, ds, slot, i).wait_send()
+            if slot % 2:
+                share(dy_all, ds, slot, i).wait_send()
+
+        @pl.when(pair > 0)
+        def _():
+            for off in range(1, replicas):
+                share(dy_all, ds, 2 * off, i).wait_send()
+
+        @pl.when(pair == 1)
+        def _():
+            for off in range(1, replicas):
+                send_across(off, i).wait_send()
 
         @pl.when(pair < last)
         def _():
@@ -467,6 +511,7 @@
             dma((2 * micro,)),
             dma((chunks,)),
             dma((chunks,)),
+            dma((replicas, chunks)),
             dma((slots, chunks)),
             dma((slots, chunks)),
             dma((slots, chunks)),

time: 82.4 us -> 81.6 us (level)
  no operation moved by 1% of the time
where the time goes in v7:
time: 81.6 us; the launch traced here: 81.5 us
  Pallas kernels  80.8 us (99%)
    pallas_call x1, Pallas kernels, body(): pl.pallas_call(functools.partial(kernel, segments, replicas, loss_scale),...  78.6 us
    pallas_call x1, Pallas kernels, body(): pl.pallas_call(hand_over, out_shape=tuple((jax.ShapeDtypeStruct(g.shape,...  2.2 us

profile of v7, /device:TPU:0, one launch (start us, length us, event | category | flops | bytes accessed | tf_op | source)
XLA Modules:
  0.0 81.5 jit_solution(11136178160405126513)
XLA Ops:
  0.6 78.6 %relay.1 = (f32[256,512]{1,0:T(8,128)}, f32[512,256]{1,0:T(8,128)}, f32[1,128]{1,0:T(1,128)}) custom-call(bf16[4,64,512]{2,1,0:T(8,128)(2,1)} %rising.1, bf16[4,64,512]{2,1,0:T(8,128)(2,1)} %falling.1, bf16[2,512,1024]{2,1,0:T(8,128)(2,1)} %up_hbm.1, bf16[2,1024,512]{2,1,0:T(8,128)(2,1)} %down_hbm.1, f32[2,512]{1,0:T(2,128)} %gain_hbm.1), custom_call_target="tpu_custom_call" | custom-call | flops 2147483648 | bytes 6291456 | tf_op jit(solution)/shard_map/relay/pallas_call | solution.py:477
  79.3 2.2 %hand_over.1 = (f32[256,512]{1,0:T(8,128)}, f32[512,256]{1,0:T(8,128)}, f32[1,128]{1,0:T(1,128)}) custom-call(f32[256,512]{1,0:T(8,128)} %get-tuple-element.6.refs_0_, f32[512,256]{1,0:T(8,128)} %get-tuple-element.7.refs_1_, f32[1,128]{1,0:T(1,128)} %get-tuple-element.8.refs_2_), custom_call_target="tpu_custom_call" | custom-call | tf_op jit(solution)/shard_map/hand_over/pallas_call | solution.py:532

commit v8 on v7

--- a/solution.py
+++ b/solution.py
@@ -10,7 +10,7 @@
 
 GELU_C = 0.7978845608028654
 CUBIC = 0.044715
-CHUNKS_PER_RELAY = 4
+CHUNKS_PER_RELAY = 2
 LAG = 3
 TILE = 256
 MESH = pl.DeviceIdType.MESH

time: 81.6 us -> 83.2 us (1.020)
  Pallas kernels: 80.8 us -> 82.4 us
    pallas_call x1, Pallas kernels: 78.6 us -> 80.2 us  [body(): pl.pallas_call(functools.partial(kernel, segments, replicas, loss_scale),...]
where the time goes in v8:
time: 83.2 us; the launch traced here: 83.1 us
  Pallas kernels  82.4 us (99%)
    pallas_call x1, Pallas kernels, body(): pl.pallas_call(functools.partial(kernel, segments, replicas, loss_scale),...  80.2 us
    pallas_call x1, Pallas kernels, body(): pl.pallas_call(hand_over, out_shape=tuple((jax.ShapeDtypeStruct(g.shape,...  2.2 us

profile of v8, /device:TPU:0, one launch (start us, length us, event | category | flops | bytes accessed | tf_op | source)
XLA Modules:
  0.0 83.1 jit_solution(12851664955648738500)
XLA Ops:
  0.6 80.2 %relay.1 = (f32[256,512]{1,0:T(8,128)}, f32[512,256]{1,0:T(8,128)}, f32[1,128]{1,0:T(1,128)}) custom-call(bf16[4,64,512]{2,1,0:T(8,128)(2,1)} %rising.1, bf16[4,64,512]{2,1,0:T(8,128)(2,1)} %falling.1, bf16[2,512,1024]{2,1,0:T(8,128)(2,1)} %up_hbm.1, bf16[2,1024,512]{2,1,0:T(8,128)(2,1)} %down_hbm.1, f32[2,512]{1,0:T(2,128)} %gain_hbm.1), custom_call_target="tpu_custom_call" | custom-call | flops 2147483648 | bytes 6291456 | tf_op jit(solution)/shard_map/relay/pallas_call | solution.py:477
  80.9 2.2 %hand_over.1 = (f32[256,512]{1,0:T(8,128)}, f32[512,256]{1,0:T(8,128)}, f32[1,128]{1,0:T(1,128)}) custom-call(f32[256,512]{1,0:T(8,128)} %get-tuple-element.6.refs_0_, f32[512,256]{1,0:T(8,128)} %get-tuple-element.7.refs_1_, f32[1,128]{1,0:T(1,128)} %get-tuple-element.8.refs_2_), custom_call_target="tpu_custom_call" | custom-call | tf_op jit(solution)/shard_map/hand_over/pallas_call | solution.py:532

commit v9 on v7

--- a/solution.py
+++ b/solution.py
@@ -12,7 +12,7 @@
 CUBIC = 0.044715
 CHUNKS_PER_RELAY = 4
 LAG = 3
-TILE = 256
+TILE = 1024
 MESH = pl.DeviceIdType.MESH
 
 

time: 81.6 us -> 77.4 us (0.949)
  Pallas kernels: 80.8 us -> 76.6 us
    pallas_call x1, Pallas kernels: 78.6 us -> 74.4 us  [body(): pl.pallas_call(functools.partial(kernel, segments, replicas, loss_scale),...]
where the time goes in v9:
time: 77.4 us; the launch traced here: 77.2 us
  Pallas kernels  76.6 us (99%)
    pallas_call x1, Pallas kernels, body(): pl.pallas_call(functools.partial(kernel, segments, replicas, loss_scale),...  74.4 us
    pallas_call x1, Pallas kernels, body(): pl.pallas_call(hand_over, out_shape=tuple((jax.ShapeDtypeStruct(g.shape,...  2.2 us

profile of v9, /device:TPU:0, one launch (start us, length us, event | category | flops | bytes accessed | tf_op | source)
XLA Modules:
  0.0 77.2 jit_solution(13912140145799773300)
XLA Ops:
  0.6 74.4 %relay.1 = (f32[256,512]{1,0:T(8,128)}, f32[512,256]{1,0:T(8,128)}, f32[1,128]{1,0:T(1,128)}) custom-call(bf16[4,64,512]{2,1,0:T(8,128)(2,1)} %rising.1, bf16[4,64,512]{2,1,0:T(8,128)(2,1)} %falling.1, bf16[2,512,1024]{2,1,0:T(8,128)(2,1)} %up_hbm.1, bf16[2,1024,512]{2,1,0:T(8,128)(2,1)} %down_hbm.1, f32[2,512]{1,0:T(2,128)} %gain_hbm.1), custom_call_target="tpu_custom_call" | custom-call | flops 2147483648 | bytes 6291456 | tf_op jit(solution)/shard_map/relay/pallas_call | solution.py:477
  75.0 2.2 %hand_over.1 = (f32[256,512]{1,0:T(8,128)}, f32[512,256]{1,0:T(8,128)}, f32[1,128]{1,0:T(1,128)}) custom-call(f32[256,512]{1,0:T(8,128)} %get-tuple-element.6.refs_0_, f32[512,256]{1,0:T(8,128)} %get-tuple-element.7.refs_1_, f32[1,128]{1,0:T(1,128)} %get-tuple-element.8.refs_2_), custom_call_target="tpu_custom_call" | custom-call | tf_op jit(solution)/shard_map/hand_over/pallas_call | solution.py:532
